TPU v7x, 32 devices: a whole 2x2x4 slice. The times are simulated.
32 devices in a mesh: row: 4 (over y, x), col: 8 (over z, core).
Axes of the slice: x: 2, y: 2, z: 4, core: 2. Of those that a mesh axis runs over, the one named last changes fastest.
Arguments:
- r_vector: bfloat16 [3072, 18432], P(('row', 'col')), may hold values from -100 to 100, as said below
- r_previous: bfloat16 [3072, 18432], P(('row', 'col')), may hold values from -100 to 100, as said below
- cycle_block: bfloat16 [18432, 18432], P('row', 'col'), may hold values from -0.046875 to 0.046875
- ladder_block: bfloat16 [48, 48, 48, 48], P(None, 'col', None, 'row'), may hold values from -0.125 to 0.125
- occ_energy: float32 [48], replicated, may hold values from -3 to -0.5
- vir_energy: float32 [384], replicated, may hold values from 0.3 to 4
- beta_previous: float32 [64], replicated, may hold values from 0.3 to 3
Outputs:
- next_vector: bfloat16 [3072, 18432], P(('row', 'col'))
- alpha_coef: float32 [64], replicated
- beta_coef: float32 [64], replicated
Inputs may be any that keep to these rules, and one draw needn't show every extreme that they name: `r_vector`: real-valued amplitudes, rough from entry to entry. `r_previous`: real-valued amplitudes, rough from entry to entry.
All inputs are finite; a program needn't handle non-finite values.
Results may differ from a plain program's by a relative error of at most 0.001.
Values may be sent and summed in bfloat16 or wider, within the bound.
No kernel may reach another device: no remote copies, remote signals or barrier semaphores. Data moves between devices by JAX's collectives and lax.ppermute only.
A program may use at most 192 MiB of HBM per device.

v0:
```python
import jax
import jax.numpy as jnp
from jax import lax
from jax.sharding import PartitionSpec as P

O = 48
V = 384
NVEC = 64


def on_device(
    r_vector, r_previous, cycle_block, ladder_block, occ_energy, vir_energy, beta_previous
):
    n_row = lax.axis_size("row")
    n_col = lax.axis_size("col")
    local_rows = r_vector.shape[0]
    row_width = r_vector.shape[1]
    all_rows = NVEC * O
    j_part = ladder_block.shape[1]
    q_part = ladder_block.shape[3]
    column_part = lax.all_to_all(r_vector, "row", split_axis=1, concat_axis=0, tiled=True)
    shaped = column_part.reshape(n_row, 1, local_rows, column_part.shape[1])
    gathered = lax.all_gather(shaped, "col", axis=1, tiled=True)
    operand = gathered.reshape(all_rows, column_part.shape[1])
    cycle_part = jnp.dot(operand, cycle_block, preferred_element_type=jnp.float32)
    ladder_part = jnp.einsum(
        "ijpq,npqa->nija",
        ladder_block,
        operand.reshape(NVEC, O, q_part, V),
        preferred_element_type=jnp.float32,
    )
    out_width = j_part * V
    partial_value = cycle_part + ladder_part.reshape(all_rows, out_width)
    summed = lax.psum_scatter(
        partial_value.reshape(n_row, n_col, local_rows, out_width),
        "row",
        scatter_dimension=0,
        tiled=True,
    )
    sigma_rows = lax.all_to_all(summed, "col", split_axis=1, concat_axis=3, tiled=True)
    sigma_rows = sigma_rows.reshape(local_rows, row_width)
    linear_index = lax.axis_index("row") * n_col + lax.axis_index("col")
    row_ids = linear_index * local_rows + jnp.arange(local_rows, dtype=jnp.int32)
    occ_index = row_ids % O
    vec_of_row = row_ids // O
    occ_rows = jnp.sum(
        jnp.where(occ_index[:, None] == jnp.arange(O)[None, :], occ_energy[None, :], 0.0), axis=1
    )
    r_float = r_vector.astype(jnp.float32)
    prev_float = r_previous.astype(jnp.float32)
    diagonal = vir_energy[None, None, :] - occ_rows[:, None, None] - occ_energy[None, :, None]
    sigma_rows = sigma_rows + (diagonal * r_float.reshape(local_rows, O, V)).reshape(
        local_rows, row_width
    )
    member = (vec_of_row[:, None] == jnp.arange(NVEC)[None, :]).astype(jnp.float32)
    count_all = O * O * V

    def per_vector(row_sums):
        return jnp.sum(member * row_sums[:, None], axis=0)

    def per_row(coefs):
        return jnp.sum(member * coefs[None, :], axis=1)

    ss_sum, rs_sum, rr_sum, sp_sum, rp_sum, pp_sum = lax.psum(
        (
            per_vector(jnp.sum(sigma_rows * sigma_rows, axis=1)),
            per_vector(jnp.sum(r_float * sigma_rows, axis=1)),
            per_vector(jnp.sum(r_float * r_float, axis=1)),
            per_vector(jnp.sum(prev_float * sigma_rows, axis=1)),
            per_vector(jnp.sum(r_float * prev_float, axis=1)),
            per_vector(jnp.sum(prev_float * prev_float, axis=1)),
        ),
        ("row", "col"),
    )
    alpha_coef = rs_sum / count_all / (rr_sum / count_all + 1e-06)
    norm_sum = (
        ss_sum
        - 2.0 * alpha_coef * rs_sum
        - 2.0 * beta_previous * sp_sum
        + alpha_coef * alpha_coef * rr_sum
        + 2.0 * alpha_coef * beta_previous * rp_sum
        + beta_previous * beta_previous * pp_sum
    )
    residual_vec = (
        sigma_rows
        - per_row(alpha_coef)[:, None] * r_float
        - per_row(beta_previous)[:, None] * prev_float
    )
    beta_coef = jnp.sqrt(norm_sum / count_all + 1e-06)
    next_vector = (residual_vec / per_row(beta_coef)[:, None]).astype(jnp.bfloat16)
    return (next_vector, alpha_coef, beta_coef)


def solution(mesh):
    placed = (
        P(("row", "col"), None),
        P(("row", "col"), None),
        P("row", "col"),
        P(None, "col", None, "row"),
        P(),
        P(),
        P(),
    )
    return jax.shard_map(
        on_device,
        mesh=mesh,
        in_specs=placed,
        out_specs=(P(("row", "col"), None), P(), P()),
        check_vma=False,
    )
```

profile of v0, /device:TPU:0, one launch (start us, length us, event | category | flops | bytes accessed | tf_op | source)
XLA Modules:
  0.0 982.2 jit_solution(16356032736975448925)
XLA Ops:
  7.2 2.3 copy.57
  9.6 45.8 %all_to_all.31 = bf16[96,4,4608]{2,0,1:T(8,128)(2,1)S(1)} all-to-all(bf16[96,4,4608]{2,0,1:T(8,128)(2,1)S(1)} %bitcast.43), channel_id=1, replica_groups=mesh['row'=4,'col'=8] {'row'}, dimensions={1} | all-to-all | bytes 7077888 | tf_op jit(solution)/shard_map/all_to_all | solution.py:21
  55.4 4.5 copy.36
  60.0 245.5 %all-gather.3.cloned.1.call-done = bf16[4,768,4608]{2,0,1:T(4,128)(2,1)} async-done(((bf16[4,96,4608]{2,0,1:T(4,128)(2,1)}), bf16[4,768,4608]{2,0,1:T(4,128)(2,1)}) %all-gather.3.cloned.1.call-update) | async-done | bytes 28311568 | tf_op jit(solution)/shard_map/all_gather | solution.py:23
  305.4 19.2 %copy.37 = bf16[4,768,4608]{2,1,0:T(8,128)(2,1)} copy(bf16[4,768,4608]{2,0,1:T(4,128)(2,1)} %all-gather.3.cloned.1.call-done) | data formatting | bytes 56623104 | tf_op jit(solution)/shard_map/all_gather | solution.py:23
  324.6 48.0 %reshape_reshape.3 = bf16[64,48,12,384]{3,2,1,0:T(8,128)(2,1)} reshape(bf16[4,768,4608]{2,1,0:T(8,128)(2,1)} %copy.37) | data formatting | bytes 56623104 | tf_op jit(solution)/shard_map/reshape;reshape | solution.py:29
  372.6 28.4 %fusion.2 = f32[64,48,6,384]{3,1,2,0:T(8,128)} fusion(bf16[64,48,12,384,1]{3,2,1,0,4:T(8,128)(2,1)} %bitcast.35, bf16[48,6,48,12]{2,0,3,1:T(8,128)(2,1)S(1)} %copy-done), kind=kOutput, calls=%fused_computation.8 | convolution fusion | flops 8153726976 | bytes 56954880 | tf_op jit(solution)/shard_map/ijpq,npqa->nija/dot_general | solution.py:26
  401.0 19.2 %copy.40 = f32[64,48,6,384]{3,2,1,0:T(8,128)S(1)} copy(f32[64,48,6,384]{3,1,2,0:T(8,128)} %fusion.2) | data formatting | bytes 56623104 | tf_op jit(solution)/shard_map/ijpq,npqa->nija/transpose | solution.py:26
  420.2 11.7 %copy.48 = f32[384,8,6,384]{3,1,2,0:T(8,128)} copy(f32[384,8,6,384]{3,2,1,0:T(8,128)S(1)} %bitcast.33) | data formatting | bytes 56623104
  431.9 78.7 %convolution_add_fusion = f32[3072,2304]{1,0:T(8,128)} fusion(f32[3072,2304]{1,0:T(8,128)} %bitcast.41, bf16[3072,4608]{1,0:T(8,128)(2,1)} %bitcast.34, bf16[4608,2304]{1,0:T(8,128)(2,1)} %param.9), kind=kOutput, calls=%fused_computation.2 | convolution fusion | flops 65236893696 | bytes 106168320 | tf_op jit(solution)/shard_map/dot_general | solution.py:25
  510.7 245.7 %reduce-scatter.4.cloned.1.call-done = f32[1,8,96,2304]{3,2,1,0:T(8,128)} async-done(((f32[4,8,96,2304]{3,2,1,0:T(8,128)}), f32[1,8,96,2304]{3,2,1,0:T(8,128)}) %reduce-scatter.4.cloned.1.call-update) | async-done | bytes 7077904
  756.4 5.2 all-to-all-start.1
  761.8 0.5 sub.59
  762.3 5.1 copy.50
  767.4 149.7 %all-to-all-done.1 = f32[1,8,96,2304]{3,2,0,1:T(8,128)} async-done(((f32[1,8,96,2304]{3,2,0,1:T(8,128)}), f32[1,8,96,2304]{3,2,0,1:T(8,128)}, u32[]{:S(2)}, u32[]{:S(2)}) %all-to-all-start.1) | async-done | bytes 7077920 | tf_op jit(solution)/shard_map/all_to_all | solution.py:40
  917.2 3.8 copy.49
  921.0 0.2 copy-done.2
  921.2 2.1 copy-done.3
  923.3 1.0 copy-done.4
  924.3 6.3 multiply_reduce_fusion
  930.6 0.2 select_reduce_fusion.4
  930.8 36.9 %all-reduce.1 = (f32[64]{0:T(128)S(1)}, f32[64]{0:T(128)S(1)}, f32[64]{0:T(128)S(1)}, f32[64]{0:T(128)S(1)}, f32[64]{0:T(128)S(1)}, /*index=5*/f32[64]{0:T(128)S(1)}) all-reduce(f32[64]{0:T(128)S(1)} %get-tuple-element.16, f32[64]{0:T(128)S(1)} %get-tuple-element.17, ...), channel_id=1, replica_groups=mesh['row'=4,'col'=8] {'row','col'}, use_global_device_ids=true, to_apply=%region_7.8 | all-reduce | flops 384 | bytes 3072 | tf_op jit(solution)/shard_map/psum | solution.py:64
  967.7 0.1 select_reduce_fusion.6
  967.9 7.5 fusion.7
  (27 shorter events, 0.4 us)
Async XLA Ops:
  7.2 365.5 %copy-start = (bf16[48,6,48,12]{2,0,3,1:T(8,128)(2,1)S(1)}, bf16[48,6,48,12]{2,0,3,1:T(8,128)(2,1)}, u32[]{:S(2)}) copy-start(bf16[48,6,48,12]{2,0,3,1:T(8,128)(2,1)} %param.10) | copy-start | bytes 995332
  7.2 298.3 %all-gather.3.cloned.1.call-start = ((), (), s32[]{:S(2)}) async-start(), calls=%async_computation.3 | async-start | bytes 31850496 | tf_op jit(solution)/shard_map/all_gather | solution.py:23
  59.9 696.5 %reduce-scatter.4.cloned.1.call-start = ((), (), s32[]{:S(2)}) async-start(), calls=%async_computation.4 | async-start | bytes 35389440
  756.4 5.2 copy-start.9
  756.4 5.3 copy-start.5
  756.4 160.8 %all-to-all-start.1 = ((f32[1,8,96,2304]{3,2,0,1:T(8,128)}), f32[1,8,96,2304]{3,2,0,1:T(8,128)}, u32[]{:S(2)}, u32[]{:S(2)}) async-start(f32[1,8,96,2304]{3,2,0,1:T(8,128)} %bitcast.44), calls=%async_computation.1 | async-start | bytes 14155776 | tf_op jit(solution)/shard_map/all_to_all | solution.py:40
  917.2 4.0 copy-start.2
  917.2 6.1 copy-start.3
  917.2 7.1 copy-start.4
  924.3 43.4 %copy-start.6 = (f32[64]{0:T(128)S(1)}, f32[64]{0:T(128)}, u32[]{:S(2)}) copy-start(f32[64]{0:T(128)} %param.13) | copy-start | bytes 772
  967.7 7.7 copy-start.7
  967.7 7.7 copy-start.8
  967.8 7.5 copy-start.1
Sparse Core Ops, SparseCore 0:
  60.0 245.3 all-gather.2
  510.8 245.5 reduce-scatter.3
where the time goes:
time: 985 us; the launch traced here: 982 us
  waiting for transfers between devices  641 us (65%)
  local copies, waits for them, and re-layouts  118 us (12%)
  matrix products  107 us (11%)
  blocking collectives  82.7 us (8%)
  other arithmetic  14.3 us (1%)
  between operations  14.2 us (1%)
    unnamed x3, waiting for transfers between devices  246 us
    all_gather x1, waiting for transfers between devices, on_device(): gathered = lax.all_gather(shaped, 'col', axis=1, tiled=True)  245 us
    all_to_all x1, waiting for transfers between devices, on_device(): lax.all_to_all(summed, 'col', split_axis=1, concat_axis=3, tiled=True)  150 us
    dot_general x1, matrix products, on_device(): jnp.dot(operand, cycle_block, preferred_element_type=jnp.float32)  78.7 us
    another operation x1, local copies, waits for them, and re-layouts, on_device(): operand.reshape(NVEC, O, q_part, V)  48 us
    all_to_all x1, blocking collectives, on_device(): lax.all_to_all(r_vector, 'row', split_axis=1, concat_axis=0, tiled=True)  45.8 us
    psum x1, blocking collectives, on_device(): lax.psum((per_vector(jnp.sum(sigma_rows * sigma_rows, axis=1)), per_vecto...  36.9 us
    dot_general x1, matrix products, on_device(): jnp.einsum('ijpq,npqa->nija', ladder_block, operand.reshape(NVEC, O, q_pa...  28.4 us
  transfers between devices with their start and end apart: 3, of which 3 were waited for; matrix products, arithmetic and copies ran while one was open for 1% of the time, Pallas kernels for 0%

commit v1 on v0

--- a/solution.py
+++ b/solution.py
@@ -1,14 +1,233 @@
+import functools
+
 import jax
 import jax.numpy as jnp
 from jax import lax
+from jax.experimental import pallas as pl
+from jax.experimental.pallas import tpu as pltpu
 from jax.sharding import PartitionSpec as P
 
 O = 48
 V = 384
 NVEC = 64
-
-
-def on_device(
+CORES = 2
+AXES = ("row", "col")
+POWER = 16
+FLOOR = 2.0**-7.75
+PART_GAIN = 16.0
+SUM_GAIN = 8.0
+
+
+def encode(value, gain):
+    size = jnp.abs(value) * gain + FLOOR
+    size = size * size
+    size = size * size
+    size = size * size
+    size = size * size
+    return jnp.where(value < 0, -size, size).astype(jnp.bfloat16)
+
+
+def decode(code, gain):
+    wide = code.astype(jnp.float32)
+    size = (jnp.exp2(jnp.log2(jnp.abs(wide)) * (1.0 / POWER)) - FLOOR) * (1.0 / gain)
+    return jnp.where(wide < 0, -size, size)
+
+
+def product_kernel(coded, mine_ref, other_ref, cycle_ref, ladder_ref, out_ref, rows_buf, ladder_buf, sems):
+    step = pl.program_id(0)
+    half, depth = mine_ref.shape
+    vectors = 2 * half // O
+    width = cycle_ref.shape[1]
+    q_part = depth // V
+    j_part = ladder_ref.shape[0] // O
+
+    @pl.when(step == 0)
+    def _():
+        first = pltpu.make_async_copy(mine_ref, rows_buf.at[pl.ds(0, half)], sems.at[0])
+        second = pltpu.make_async_copy(other_ref, rows_buf.at[pl.ds(half, half)], sems.at[1])
+        first.start()
+        second.start()
+        first.wait()
+        second.wait()
+        for n in range(vectors):
+            stacked = jnp.concatenate(
+                [rows_buf[n * O : (n + 1) * O, q * V : (q + 1) * V] for q in range(q_part)], axis=0
+            )
+            term = jnp.dot(ladder_ref[...], stacked, preferred_element_type=jnp.float32)
+            for j in range(j_part):
+                ladder_buf[n * O : (n + 1) * O, j * V : (j + 1) * V] = term[j * O : (j + 1) * O]
+
+    start = pl.multiple_of(step * width, width)
+    value = jnp.dot(rows_buf[...], cycle_ref[...], preferred_element_type=jnp.float32)
+    value = value + ladder_buf[:, pl.ds(start, width)]
+    if coded:
+        out_ref[...] = encode(value, PART_GAIN)
+    else:
+        out_ref[...] = value
+
+
+def product(mine, other, cycle_block, ladder_rows, coded):
+    half, depth = mine.shape
+    out_width = cycle_block.shape[1]
+    width = 2 * V if out_width % (2 * V) == 0 else V
+    flops = 2 * 2 * half * depth * out_width
+    return pl.pallas_call(
+        functools.partial(product_kernel, coded),
+        grid=(out_width // width,),
+        in_specs=[
+            pl.BlockSpec(memory_space=pl.ANY),
+            pl.BlockSpec(memory_space=pl.ANY),
+            pl.BlockSpec((depth, width), lambda i: (0, i)),
+            pl.BlockSpec(ladder_rows.shape, lambda i: (0, 0)),
+        ],
+        out_specs=pl.BlockSpec((2 * half, width), lambda i: (0, i)),
+        out_shape=jax.ShapeDtypeStruct((2 * half, out_width), jnp.bfloat16 if coded else jnp.float32),
+        scratch_shapes=[
+            pltpu.VMEM((2 * half, depth), jnp.bfloat16),
+            pltpu.VMEM((2 * half, out_width), jnp.float32),
+            pltpu.SemaphoreType.DMA((2,)),
+        ],
+        compiler_params=pltpu.CompilerParams(vmem_limit_bytes=40 * 1024 * 1024),
+        cost_estimate=pl.CostEstimate(
+            flops=flops, bytes_accessed=2 * depth * out_width, transcendentals=0
+        ),
+    )(mine, other, cycle_block, ladder_rows)
+
+
+def power_of_two(exponent):
+    return jnp.exp2(exponent).astype(jnp.bfloat16)
+
+
+def streamed(
+    r_vector, r_previous, cycle_block, ladder_block, occ_energy, vir_energy, beta_previous
+):
+    n_row = lax.axis_size("row")
+    n_col = lax.axis_size("col")
+    n_chip = n_col // CORES
+    local_rows, row_width = r_vector.shape
+    depth = row_width // n_row
+    out_width = cycle_block.shape[1]
+    j_part = ladder_block.shape[1]
+    q_part = ladder_block.shape[3]
+    row_at = lax.axis_index("row")
+    col_at = lax.axis_index("col")
+    chip_at = col_at // CORES
+    core_at = col_at % CORES
+    order = list(range(0, n_chip, 2)) + list(range(1, n_chip, 2))[::-1]
+    place = [order.index(chip) for chip in range(n_chip)]
+    paired = n_row & (n_row - 1) == 0
+
+    def partner(row, m):
+        return row ^ m if paired else (row + m) % n_row
+
+    def back(row, m):
+        return row ^ m if paired else (row + n_row - m) % n_row
+
+    def send(value, rows=0, hops=0, swap=0, reverse=False):
+        pairs = []
+        for row in range(n_row):
+            for chip in range(n_chip):
+                for core in range(CORES):
+                    to_row = back(row, rows) if reverse else partner(row, rows)
+                    to_chip = order[(place[chip] + hops) % n_chip]
+                    to_core = (core + swap) % CORES
+                    pairs.append(
+                        (
+                            row * n_col + chip * CORES + core,
+                            to_row * n_col + to_chip * CORES + to_core,
+                        )
+                    )
+        return lax.ppermute(value, AXES, pairs)
+
+    ladder_rows = ladder_block.transpose(1, 0, 3, 2).reshape(j_part * O, q_part * O)
+
+    vectors = local_rows // O
+    r_float = r_vector.astype(jnp.float32)
+    rr_sum = jnp.sum(r_float.reshape(vectors, O * row_width) ** 2, axis=1)
+    exponent = jnp.clip(jnp.floor(0.5 * jnp.log2(jnp.maximum(rr_sum, 1e-37))), -60.0, 60.0)
+    shrink = jnp.repeat(power_of_two(-exponent), O)
+    grow = jnp.repeat(power_of_two(exponent), O).astype(jnp.float32)
+
+    def own_part(m):
+        at = partner(row_at, m) * depth
+        return lax.dynamic_slice_in_dim(r_vector, at, depth, axis=1) * shrink[:, None]
+
+    held = [own_part(0)]
+    for m in range(1, n_row):
+        held.append(send(own_part(m), rows=m))
+    received = []
+    for s in range(n_chip):
+        if s > 0:
+            held = [send(part, hops=1) for part in held]
+        turn = list(range(1, n_row)) + [0] if s > 0 else list(range(n_row))
+        total = None
+        parts = {}
+        for m in turn:
+            other = send(held[m], swap=1)
+            parts[m] = product(held[m], other, cycle_block, ladder_rows, m != 0)
+        total = parts[0]
+        for m in range(1, n_row):
+            arrived = send(parts[m], rows=m, reverse=True)
+            total = total + decode(arrived, PART_GAIN)
+        if s == 0:
+            received.append(total[:local_rows])
+            received.append(send(total[local_rows:], swap=1))
+        else:
+            code = encode(total, SUM_GAIN)
+            for swap in range(CORES):
+                block = code[swap * local_rows : (swap + 1) * local_rows]
+                received.append(decode(send(block, hops=n_chip - s, swap=swap), SUM_GAIN))
+
+    order_table = jnp.array(order, dtype=jnp.int32)
+    place_at = jnp.array(place, dtype=jnp.int32)[chip_at]
+    starts = []
+    for s in range(n_chip):
+        for swap in range(CORES):
+            chip = order_table[(place_at + s) % n_chip]
+            starts.append((chip * CORES + (core_at + swap) % CORES) * out_width)
+
+    def blocks_of(array):
+        return [lax.dynamic_slice_in_dim(array, at, out_width, axis=1) for at in starts]
+
+    r_blocks = blocks_of(r_vector)
+    prev_blocks = blocks_of(r_previous)
+    count_all = O * O * V
+    linear_index = row_at * n_col + col_at
+    occ_tile = jnp.tile(occ_energy, vectors)
+    sigma_blocks = []
+    for at, block, value in zip(starts, r_blocks, received):
+        occ_here = lax.dynamic_slice_in_dim(occ_energy, at // V, j_part)
+        diagonal = vir_energy[None, None, :] - occ_tile[:, None, None] - occ_here[None, :, None]
+        sigma_blocks.append(
+            value * grow[:, None]
+            + diagonal.reshape(local_rows, out_width) * block.astype(jnp.float32)
+        )
+
+    def per_vector(values):
+        return sum(jnp.sum(v.reshape(vectors, O * out_width), axis=1) for v in values)
+
+    rs_sum = per_vector([s * b.astype(jnp.float32) for s, b in zip(sigma_blocks, r_blocks)])
+    alpha = rs_sum / count_all / (rr_sum / count_all + 1e-06)
+    beta_here = lax.dynamic_slice_in_dim(beta_previous, linear_index * vectors, vectors)
+    alpha_rows = jnp.repeat(alpha, O)[:, None]
+    beta_rows = jnp.repeat(beta_here, O)[:, None]
+    residual = [
+        s - alpha_rows * b.astype(jnp.float32) - beta_rows * p.astype(jnp.float32)
+        for s, b, p in zip(sigma_blocks, r_blocks, prev_blocks)
+    ]
+    beta = jnp.sqrt(per_vector([v * v for v in residual]) / count_all + 1e-06)
+    next_vector = jnp.zeros((local_rows, row_width), jnp.bfloat16)
+    for at, v in zip(starts, residual):
+        next_vector = lax.dynamic_update_slice_in_dim(
+            next_vector, (v / jnp.repeat(beta, O)[:, None]).astype(jnp.bfloat16), at, axis=1
+        )
+    both = jnp.zeros((2, NVEC), jnp.float32)
+    both = lax.dynamic_update_slice(both, jnp.stack([alpha, beta]), (0, linear_index * vectors))
+    both = lax.psum(both, AXES)
+    return (next_vector, both[0], both[1])
+
+
+def gathered(
     r_vector, r_previous, cycle_block, ladder_block, occ_energy, vir_energy, beta_previous
 ):
     n_row = lax.axis_size("row")
@@ -70,7 +289,7 @@
             per_vector(jnp.sum(r_float * prev_float, axis=1)),
             per_vector(jnp.sum(prev_float * prev_float, axis=1)),
         ),
-        ("row", "col"),
+        AXES,
     )
     alpha_coef = rs_sum / count_all / (rr_sum / count_all + 1e-06)
     norm_sum = (
@@ -91,10 +310,16 @@
     return (next_vector, alpha_coef, beta_coef)
 
 
+def on_device(r_vector, *others):
+    whole_vectors = r_vector.shape[0] % O == 0 and lax.axis_size("col") % CORES == 0
+    body = streamed if whole_vectors else gathered
+    return body(r_vector, *others)
+
+
 def solution(mesh):
     placed = (
-        P(("row", "col"), None),
-        P(("row", "col"), None),
+        P(AXES, None),
+        P(AXES, None),
         P("row", "col"),
         P(None, "col", None, "row"),
         P(),
@@ -105,6 +330,6 @@
         on_device,
         mesh=mesh,
         in_specs=placed,
-        out_specs=(P(("row", "col"), None), P(), P()),
+        out_specs=(P(AXES, None), P(), P()),
         check_vma=False,
     )

time: 985 us -> 561 us (0.57)
  waiting for transfers between devices: 641 us -> 146 us
  Pallas kernels: 0 us -> 187 us
  matrix products: 107 us -> 0 us
  local copies, waits for them, and re-layouts: 118 us -> 40.7 us
  other arithmetic: 14.3 us -> 63.1 us
  starting transfers between devices: 5.26 us -> 49.7 us
  blocking collectives: 82.7 us -> 57.5 us
    unnamed x3 -> x0, waiting for transfers between devices: 246 us -> none
    all_gather x1 -> x0, waiting for transfers between devices: 245 us -> none  [on_device(): gathered = lax.all_gather(shaped, 'col', axis=1, tiled=True)]
    pallas_call x0 -> x16, Pallas kernels: none -> 187 us  [product(): pl.pallas_call(functools.partial(product_kernel, coded), grid=(out_width...]
    all_to_all x1 -> x0, waiting for transfers between devices: 150 us -> none  [on_device(): lax.all_to_all(summed, 'col', split_axis=1, concat_axis=3, tiled=True)]
    ppermute x0 -> x50, waiting for transfers between devices: none -> 146 us  [send(): return lax.ppermute(value, AXES, pairs)]
    dot_general x2 -> x0, matrix products: 107 us -> none  [the longest x1 78.7 us: on_device(): jnp.dot(operand, cycle_block, preferred_element_type=jnp.float32)]
    ppermute x0 -> x50, starting transfers between devices: none -> 49.7 us  [send(): return lax.ppermute(value, AXES, pairs)]
    another operation x1, local copies, waits for them, and re-layouts: 48 us -> 0.01 us  [streamed(): occ_tile = jnp.tile(occ_energy, vectors)]
  transfers between devices with their start and end apart: 3 -> 50, of which waited for: 3 -> 14; matrix products, arithmetic and copies ran while one was open for 1% -> 5% of each run, Pallas kernels for 0% -> 34%
where the time goes in v1:
time: 561 us; the launch traced here: 553 us
  Pallas kernels  187 us (33%)
  waiting for transfers between devices  146 us (26%)
  other arithmetic  63.1 us (11%)
  blocking collectives  57.5 us (10%)
  starting transfers between devices  49.7 us (9%)
  local copies, waits for them, and re-layouts  40.7 us (7%)
  between operations  8.72 us (2%)
    pallas_call x16, Pallas kernels, product(): pl.pallas_call(functools.partial(product_kernel, coded), grid=(out_width...  187 us
    ppermute x50, waiting for transfers between devices, send(): return lax.ppermute(value, AXES, pairs)  146 us
    psum x1, blocking collectives, streamed(): both = lax.psum(both, AXES)  57.5 us
    ppermute x50, starting transfers between devices, send(): return lax.ppermute(value, AXES, pairs)  49.7 us
    reduce_sum x20, other arithmetic, per_vector(): jnp.sum(v.reshape(vectors, O * out_width), axis=1)  37.9 us
    reduce_sum x16, local copies, waits for them, and re-layouts, per_vector(): jnp.sum(v.reshape(vectors, O * out_width), axis=1)  17.6 us
  transfers between devices with their start and end apart: 50, of which 14 were waited for; matrix products, arithmetic and copies ran while one was open for 5% of the time, Pallas kernels for 34%

profile of v1, /device:TPU:0, one launch (start us, length us, event | category | flops | bytes accessed | tf_op | source)
XLA Modules:
  0.0 552.8 jit_solution(7266657421464345239)
XLA Ops:
  15.9 16.0 %collective-permute-done.1.mine_ref = bf16[96,4608]{1,0:T(8,128)(2,1)} collective-permute-done((bf16[96,4608]{1,0:T(8,128)(2,1)S(1)}, bf16[96,4608]{1,0:T(8,128)(2,1)}, u32[]{:S(2)}, u32[]{:S(2)}) %collective-permute-start.1) | collective-permute-done | bytes 884768 | tf_op jit(solution)/shard_map/ppermute | solution.py:140
  40.3 13.7 %collective-permute-done.4.mine_ref = bf16[96,4608]{1,0:T(8,128)(2,1)} collective-permute-done((bf16[96,4608]{1,0:T(8,128)(2,1)}, bf16[96,4608]{1,0:T(8,128)(2,1)}, u32[]{:S(2)}, u32[]{:S(2)}) %collective-permute-start.4) | collective-permute-done | bytes 884768 | tf_op jit(solution)/shard_map/ppermute | solution.py:140
  65.5 12.7 %shard_map.112 = f32[192,2304]{1,0:T(8,128)S(1)} custom-call(bf16[96,4608]{1,0:T(8,128)(2,1)S(1)} %get-tuple-element.30.mine_ref, bf16[96,4608]{1,0:T(8,128)(2,1)} %collective-permute-done.other_ref, bf16[4608,2304]{1,0:T(8,128)(2,1)} %cycle_ref.31, bf16[288,576]{1,0:T(8,128)(2,1)S(1)} %reshape.269.ladder_ref), custom_call_target="tpu_custom_call" | custom-call | flops 4076863488 | bytes 21233664 | tf_op jit(solution)/shard_map/pallas_call | solution.py:74
  78.4 12.7 %shard_map.116 = f32[192,2304]{1,0:T(8,128)S(1)} custom-call(bf16[96,4608]{1,0:T(8,128)(2,1)S(1)} %collective-permute-done.11.mine_ref, bf16[96,4608]{1,0:T(8,128)(2,1)} %collective-permute-done.12.other_ref, bf16[4608,2304]{1,0:T(8,128)(2,1)} %cycle_ref.31, bf16[288,576]{1,0:T(8,128)(2,1)S(1)} %reshape.269.ladder_ref), custom_call_target="tpu_custom_call" | custom-call | flops 4076863488 | bytes 21233664 | tf_op jit(solution)/shard_map/pallas_call | solution.py:74
  93.8 13.1 %shard_map.113 = bf16[192,2304]{1,0:T(8,128)(2,1)S(1)} custom-call(bf16[96,4608]{1,0:T(8,128)(2,1)} %collective-permute-done.1.mine_ref, bf16[96,4608]{1,0:T(8,128)(2,1)} %collective-permute-done.2.other_ref, bf16[4608,2304]{1,0:T(8,128)(2,1)} %cycle_ref.31, bf16[288,576]{1,0:T(8,128)(2,1)S(1)} %reshape.269.ladder_ref), custom_call_target="tpu_custom_call" | custom-call | flops 4076863488 | bytes 21233664 | tf_op jit(solution)/shard_map/pallas_call | solution.py:74
  106.9 13.1 %shard_map.114 = bf16[192,2304]{1,0:T(8,128)(2,1)S(1)} custom-call(bf16[96,4608]{1,0:T(8,128)(2,1)} %collective-permute-done.4.mine_ref, bf16[96,4608]{1,0:T(8,128)(2,1)} %collective-permute-done.5.other_ref, bf16[4608,2304]{1,0:T(8,128)(2,1)} %cycle_ref.31, bf16[288,576]{1,0:T(8,128)(2,1)S(1)} %reshape.269.ladder_ref), custom_call_target="tpu_custom_call" | custom-call | flops 4076863488 | bytes 21233664 | tf_op jit(solution)/shard_map/pallas_call | solution.py:74
  120.7 12.8 %shard_map.115 = bf16[192,2304]{1,0:T(8,128)(2,1)S(1)} custom-call(bf16[96,4608]{1,0:T(8,128)(2,1)} %collective-permute-done.7.mine_ref, bf16[96,4608]{1,0:T(8,128)(2,1)S(1)} %collective-permute-done.8.other_ref, bf16[4608,2304]{1,0:T(8,128)(2,1)} %cycle_ref.31, bf16[288,576]{1,0:T(8,128)(2,1)S(1)} %reshape.269.ladder_ref), custom_call_target="tpu_custom_call" | custom-call | flops 4076863488 | bytes 21233664 | tf_op jit(solution)/shard_map/pallas_call | solution.py:74
  138.9 10.8 %shard_map.117 = bf16[192,2304]{1,0:T(8,128)(2,1)S(1)} custom-call(bf16[96,4608]{1,0:T(8,128)(2,1)S(1)} %collective-permute-done.13.mine_ref, bf16[96,4608]{1,0:T(8,128)(2,1)S(1)} %collective-permute-done.14.other_ref, bf16[4608,2304]{1,0:T(8,128)(2,1)} %cycle_ref.31, bf16[288,576]{1,0:T(8,128)(2,1)S(1)} %reshape.269.ladder_ref), custom_call_target="tpu_custom_call" | custom-call | flops 4076863488 | bytes 21233664 | tf_op jit(solution)/shard_map/pallas_call | solution.py:74
  149.8 12.9 %shard_map.118 = bf16[192,2304]{1,0:T(8,128)(2,1)S(1)} custom-call(bf16[96,4608]{1,0:T(8,128)(2,1)} %collective-permute-done.16.mine_ref, bf16[96,4608]{1,0:T(8,128)(2,1)S(1)} %collective-permute-done.17.other_ref, bf16[4608,2304]{1,0:T(8,128)(2,1)} %cycle_ref.31, bf16[288,576]{1,0:T(8,128)(2,1)S(1)} %reshape.269.ladder_ref), custom_call_target="tpu_custom_call" | custom-call | flops 4076863488 | bytes 21233664 | tf_op jit(solution)/shard_map/pallas_call | solution.py:74
  162.6 12.9 %shard_map.119 = bf16[192,2304]{1,0:T(8,128)(2,1)S(1)} custom-call(bf16[96,4608]{1,0:T(8,128)(2,1)} %collective-permute-done.19.mine_ref, bf16[96,4608]{1,0:T(8,128)(2,1)S(1)} %collective-permute-done.20.other_ref, bf16[4608,2304]{1,0:T(8,128)(2,1)} %cycle_ref.31, bf16[288,576]{1,0:T(8,128)(2,1)S(1)} %reshape.269.ladder_ref), custom_call_target="tpu_custom_call" | custom-call | flops 4076863488 | bytes 21233664 | tf_op jit(solution)/shard_map/pallas_call | solution.py:74
  183.7 10.7 %shard_map.120 = f32[192,2304]{1,0:T(8,128)S(1)} custom-call(bf16[96,4608]{1,0:T(8,128)(2,1)S(1)} %collective-permute-done.24.mine_ref, bf16[96,4608]{1,0:T(8,128)(2,1)S(1)} %collective-permute-done.25.other_ref, bf16[4608,2304]{1,0:T(8,128)(2,1)} %cycle_ref.31, bf16[288,576]{1,0:T(8,128)(2,1)S(1)} %reshape.269.ladder_ref), custom_call_target="tpu_custom_call" | custom-call | flops 4076863488 | bytes 21233664 | tf_op jit(solution)/shard_map/pallas_call | solution.py:74
  199.9 17.2 %collective-permute-done.37.mine_ref = bf16[96,4608]{1,0:T(8,128)(2,1)S(1)} collective-permute-done((bf16[96,4608]{1,0:T(8,128)(2,1)S(1)}, bf16[96,4608]{1,0:T(8,128)(2,1)S(1)}, u32[]{:S(2)}, u32[]{:S(2)}) %collective-permute-start.37) | collective-permute-done | bytes 884768 | tf_op jit(solution)/shard_map/ppermute | solution.py:140
  222.5 13.6 %collective-permute-done.32.mine_ref = bf16[96,4608]{1,0:T(8,128)(2,1)S(1)} collective-permute-done((bf16[96,4608]{1,0:T(8,128)(2,1)}, bf16[96,4608]{1,0:T(8,128)(2,1)S(1)}, u32[]{:S(2)}, u32[]{:S(2)}) %collective-permute-start.32) | collective-permute-done | bytes 884768 | tf_op jit(solution)/shard_map/ppermute | solution.py:140
  236.2 18.9 %collective-permute-done.39.mine_ref = bf16[96,4608]{1,0:T(8,128)(2,1)S(1)} collective-permute-done((bf16[96,4608]{1,0:T(8,128)(2,1)S(1)}, bf16[96,4608]{1,0:T(8,128)(2,1)S(1)}, u32[]{:S(2)}, u32[]{:S(2)}) %collective-permute-start.39) | collective-permute-done | bytes 884768 | tf_op jit(solution)/shard_map/ppermute | solution.py:140
  256.8 10.7 %shard_map.124 = f32[192,2304]{1,0:T(8,128)S(1)} custom-call(bf16[96,4608]{1,0:T(8,128)(2,1)S(1)} %collective-permute-done.37.mine_ref, bf16[96,4608]{1,0:T(8,128)(2,1)S(1)} %collective-permute-done.38.other_ref, bf16[4608,2304]{1,0:T(8,128)(2,1)} %cycle_ref.31, bf16[288,576]{1,0:T(8,128)(2,1)S(1)} %reshape.269.ladder_ref), custom_call_target="tpu_custom_call" | custom-call | flops 4076863488 | bytes 21233664 | tf_op jit(solution)/shard_map/pallas_call | solution.py:74
  268.1 10.8 %shard_map.121 = bf16[192,2304]{1,0:T(8,128)(2,1)S(1)} custom-call(bf16[96,4608]{1,0:T(8,128)(2,1)S(1)} %collective-permute-done.26.mine_ref, bf16[96,4608]{1,0:T(8,128)(2,1)S(1)} %collective-permute-done.27.other_ref, bf16[4608,2304]{1,0:T(8,128)(2,1)} %cycle_ref.31, bf16[288,576]{1,0:T(8,128)(2,1)S(1)} %reshape.269.ladder_ref), custom_call_target="tpu_custom_call" | custom-call | flops 4076863488 | bytes 21233664 | tf_op jit(solution)/shard_map/pallas_call | solution.py:74
  280.4 10.8 %shard_map.122 = bf16[192,2304]{1,0:T(8,128)(2,1)S(1)} custom-call(bf16[96,4608]{1,0:T(8,128)(2,1)S(1)} %collective-permute-done.29.mine_ref, bf16[96,4608]{1,0:T(8,128)(2,1)S(1)} %collective-permute-done.30.other_ref, bf16[4608,2304]{1,0:T(8,128)(2,1)} %cycle_ref.31, bf16[288,576]{1,0:T(8,128)(2,1)S(1)} %reshape.269.ladder_ref), custom_call_target="tpu_custom_call" | custom-call | flops 4076863488 | bytes 21233664 | tf_op jit(solution)/shard_map/pallas_call | solution.py:74
  294.6 10.8 %shard_map.123 = bf16[192,2304]{1,0:T(8,128)(2,1)S(1)} custom-call(bf16[96,4608]{1,0:T(8,128)(2,1)S(1)} %collective-permute-done.32.mine_ref, bf16[96,4608]{1,0:T(8,128)(2,1)S(1)} %collective-permute-done.33.other_ref, bf16[4608,2304]{1,0:T(8,128)(2,1)} %cycle_ref.31, bf16[288,576]{1,0:T(8,128)(2,1)S(1)} %reshape.269.ladder_ref), custom_call_target="tpu_custom_call" | custom-call | flops 4076863488 | bytes 21233664 | tf_op jit(solution)/shard_map/pallas_call | solution.py:74
  306.0 10.8 %shard_map.125 = bf16[192,2304]{1,0:T(8,128)(2,1)S(1)} custom-call(bf16[96,4608]{1,0:T(8,128)(2,1)S(1)} %collective-permute-done.39.mine_ref, bf16[96,4608]{1,0:T(8,128)(2,1)S(1)} %collective-permute-done.40.other_ref, bf16[4608,2304]{1,0:T(8,128)(2,1)} %cycle_ref.31, bf16[288,576]{1,0:T(8,128)(2,1)S(1)} %reshape.269.ladder_ref), custom_call_target="tpu_custom_call" | custom-call | flops 4076863488 | bytes 21233664 | tf_op jit(solution)/shard_map/pallas_call | solution.py:74
  317.1 11.0 %shard_map.126 = bf16[192,2304]{1,0:T(8,128)(2,1)S(1)} custom-call(bf16[96,4608]{1,0:T(8,128)(2,1)S(1)} %collective-permute-done.42.mine_ref, bf16[96,4608]{1,0:T(8,128)(2,1)S(1)} %collective-permute-done.43.other_ref, bf16[4608,2304]{1,0:T(8,128)(2,1)} %cycle_ref.31, bf16[288,576]{1,0:T(8,128)(2,1)S(1)} %reshape.269.ladder_ref), custom_call_target="tpu_custom_call" | custom-call | flops 4076863488 | bytes 21233664 | tf_op jit(solution)/shard_map/pallas_call | solution.py:74
  328.7 10.8 %shard_map.127 = bf16[192,2304]{1,0:T(8,128)(2,1)S(1)} custom-call(bf16[96,4608]{1,0:T(8,128)(2,1)S(1)} %collective-permute-done.45.mine_ref, bf16[96,4608]{1,0:T(8,128)(2,1)S(1)} %collective-permute-done.46.other_ref, bf16[4608,2304]{1,0:T(8,128)(2,1)} %cycle_ref.31, bf16[288,576]{1,0:T(8,128)(2,1)S(1)} %reshape.269.ladder_ref), custom_call_target="tpu_custom_call" | custom-call | flops 4076863488 | bytes 21233664 | tf_op jit(solution)/shard_map/pallas_call | solution.py:74
  346.0 16.1 %collective-permute-done.41 = bf16[192,2304]{1,0:T(8,128)(2,1)S(1)} collective-permute-done((bf16[192,2304]{1,0:T(8,128)(2,1)S(1)}, bf16[192,2304]{1,0:T(8,128)(2,1)S(1)}, u32[]{:S(2)}, u32[]{:S(2)}) %collective-permute-start.41) | collective-permute-done | bytes 884768 | tf_op jit(solution)/shard_map/ppermute | solution.py:140
  362.1 19.1 %collective-permute-done.44 = bf16[192,2304]{1,0:T(8,128)(2,1)S(1)} collective-permute-done((bf16[192,2304]{1,0:T(8,128)(2,1)S(1)}, bf16[192,2304]{1,0:T(8,128)(2,1)S(1)}, u32[]{:S(2)}, u32[]{:S(2)}) %collective-permute-start.44) | collective-permute-done | bytes 884768 | tf_op jit(solution)/shard_map/ppermute | solution.py:140
  483.9 57.5 %psum.7 = f32[2,64]{1,0:T(2,128)S(1)} all-reduce(f32[2,64]{1,0:T(2,128)S(1)} %dynamic_update_slice.35), channel_id=1, replica_groups=mesh['row'=4,'col'=8] {'row','col'}, use_global_device_ids=true, to_apply=%region_34.35 | all-reduce | flops 128 | bytes 1024 | tf_op jit(solution)/shard_map/psum | solution.py:226
  (246 shorter events, 184.7 us)
Async XLA Ops:
  13.9 40.1 %collective-permute-start.4 = (bf16[96,4608]{1,0:T(8,128)(2,1)}, bf16[96,4608]{1,0:T(8,128)(2,1)}, u32[]{:S(2)}, u32[]{:S(2)}) collective-permute-start(bf16[96,4608]{1,0:T(8,128)(2,1)} %get-tuple-element.28), channel_id=1, source_target_pairs={{0,16},{1,17},{2,18},{3,19},{4,20},{5,21},{6,22},{7,23},{8,24},{9,... | collective-permute-start | bytes 2654216 | tf_op jit(solution)/shard_map/ppermute | solution.py:140
  15.4 40.2 %collective-permute-start.7 = (bf16[96,4608]{1,0:T(8,128)(2,1)}, bf16[96,4608]{1,0:T(8,128)(2,1)}, u32[]{:S(2)}, u32[]{:S(2)}) collective-permute-start(bf16[96,4608]{1,0:T(8,128)(2,1)} %get-tuple-element.27), channel_id=1, source_target_pairs={{0,24},{1,25},{2,26},{3,27},{4,28},{5,29},{6,30},{7,31},{8,16},{9,... | collective-permute-start | bytes 2654216 | tf_op jit(solution)/shard_map/ppermute | solution.py:140
  15.9 40.0 %collective-permute-start = (bf16[96,4608]{1,0:T(8,128)(2,1)S(1)}, bf16[96,4608]{1,0:T(8,128)(2,1)}, u32[]{:S(2)}, u32[]{:S(2)}) collective-permute-start(bf16[96,4608]{1,0:T(8,128)(2,1)S(1)} %get-tuple-element.30.mine_ref), channel_id=1, source_target_pairs={{0,1},{1,0},{2,3},{3,2},{4,5},{5,4},{6,7},{7,6},{8,9},{9,8},{10,11... | collective-permute-start | bytes 2654216 | tf_op jit(solution)/shard_map/ppermute | solution.py:140
  35.1 43.1 %collective-permute-start.12 = (bf16[96,4608]{1,0:T(8,128)(2,1)S(1)}, bf16[96,4608]{1,0:T(8,128)(2,1)}, u32[]{:S(2)}, u32[]{:S(2)}) collective-permute-start(bf16[96,4608]{1,0:T(8,128)(2,1)S(1)} %collective-permute-done.11.mine_ref), channel_id=1, source_target_pairs={{0,1},{1,0},{2,3},{3,2},{4,5},{5,4},{6,7},{7,6},{8,9},{9,8},{10,11... | collective-permute-start | bytes 2654216 | tf_op jit(solution)/shard_map/ppermute | solution.py:140
  78.2 41.8 %collective-permute-start.8 = (bf16[96,4608]{1,0:T(8,128)(2,1)}, bf16[96,4608]{1,0:T(8,128)(2,1)S(1)}, u32[]{:S(2)}, u32[]{:S(2)}) collective-permute-start(bf16[96,4608]{1,0:T(8,128)(2,1)} %collective-permute-done.7.mine_ref), channel_id=1, source_target_pairs={{0,1},{1,0},{2,3},{3,2},{4,5},{5,4},{6,7},{7,6},{8,9},{9,8},{10,11... | collective-permute-start | bytes 2654216 | tf_op jit(solution)/shard_map/ppermute | solution.py:140
  91.1 42.5 %collective-permute-start.24 = (bf16[96,4608]{1,0:T(8,128)(2,1)S(1)}, bf16[96,4608]{1,0:T(8,128)(2,1)S(1)}, u32[]{:S(2)}, u32[]{:S(2)}) collective-permute-start(bf16[96,4608]{1,0:T(8,128)(2,1)S(1)} %collective-permute-done.11.mine_ref), channel_id=1, source_target_pairs={{0,4},{1,5},{2,0},{3,1},{4,6},{5,7},{6,2},{7,3},{8,12},{9,13},{10,... | collective-permute-start | bytes 2654216 | tf_op jit(solution)/shard_map/ppermute | solution.py:140
  93.2 42.0 %collective-permute-start.14 = (bf16[96,4608]{1,0:T(8,128)(2,1)S(1)}, bf16[96,4608]{1,0:T(8,128)(2,1)S(1)}, u32[]{:S(2)}, u32[]{:S(2)}) collective-permute-start(bf16[96,4608]{1,0:T(8,128)(2,1)S(1)} %collective-permute-done.13.mine_ref), channel_id=1, source_target_pairs={{0,1},{1,0},{2,3},{3,2},{4,5},{5,4},{6,7},{7,6},{8,9},{9,8},{10,11... | collective-permute-start | bytes 2654216 | tf_op jit(solution)/shard_map/ppermute | solution.py:140
  93.2 43.3 %collective-permute-start.17 = (bf16[96,4608]{1,0:T(8,128)(2,1)}, bf16[96,4608]{1,0:T(8,128)(2,1)S(1)}, u32[]{:S(2)}, u32[]{:S(2)}) collective-permute-start(bf16[96,4608]{1,0:T(8,128)(2,1)} %collective-permute-done.16.mine_ref), channel_id=1, source_target_pairs={{0,1},{1,0},{2,3},{3,2},{4,5},{5,4},{6,7},{7,6},{8,9},{9,8},{10,11... | collective-permute-start | bytes 2654216 | tf_op jit(solution)/shard_map/ppermute | solution.py:140
  93.7 45.2 %collective-permute-start.20 = (bf16[96,4608]{1,0:T(8,128)(2,1)}, bf16[96,4608]{1,0:T(8,128)(2,1)S(1)}, u32[]{:S(2)}, u32[]{:S(2)}) collective-permute-start(bf16[96,4608]{1,0:T(8,128)(2,1)} %collective-permute-done.19.mine_ref), channel_id=1, source_target_pairs={{0,1},{1,0},{2,3},{3,2},{4,5},{5,4},{6,7},{7,6},{8,9},{9,8},{10,11... | collective-permute-start | bytes 2654216 | tf_op jit(solution)/shard_map/ppermute | solution.py:140
  120.0 56.7 %collective-permute-start.3 = (bf16[192,2304]{1,0:T(8,128)(2,1)S(1)}, bf16[192,2304]{1,0:T(8,128)(2,1)S(1)}, u32[]{:S(2)}, u32[]{:S(2)}) collective-permute-start(bf16[192,2304]{1,0:T(8,128)(2,1)S(1)} %shard_map.113), channel_id=1, source_target_pairs={{0,8},{1,9},{2,10},{3,11},{4,12},{5,13},{6,14},{7,15},{8,0},{9,1},... | collective-permute-start | bytes 2654216 | tf_op jit(solution)/shard_map/ppermute | solution.py:140
  133.6 44.3 %collective-permute-start.6 = (bf16[192,2304]{1,0:T(8,128)(2,1)S(1)}, bf16[192,2304]{1,0:T(8,128)(2,1)S(1)}, u32[]{:S(2)}, u32[]{:S(2)}) collective-permute-start(bf16[192,2304]{1,0:T(8,128)(2,1)S(1)} %shard_map.114), channel_id=1, source_target_pairs={{0,16},{1,17},{2,18},{3,19},{4,20},{5,21},{6,22},{7,23},{8,24},{9,... | collective-permute-start | bytes 2654216 | tf_op jit(solution)/shard_map/ppermute | solution.py:140
  135.2 44.2 %collective-permute-start.9 = (bf16[192,2304]{1,0:T(8,128)(2,1)S(1)}, bf16[192,2304]{1,0:T(8,128)(2,1)S(1)}, u32[]{:S(2)}, u32[]{:S(2)}) collective-permute-start(bf16[192,2304]{1,0:T(8,128)(2,1)S(1)} %shard_map.115), channel_id=1, source_target_pairs={{0,24},{1,25},{2,26},{3,27},{4,28},{5,29},{6,30},{7,31},{8,16},{9,... | collective-permute-start | bytes 2654216 | tf_op jit(solution)/shard_map/ppermute | solution.py:140
  176.4 40.8 %collective-permute-start.37 = (bf16[96,4608]{1,0:T(8,128)(2,1)S(1)}, bf16[96,4608]{1,0:T(8,128)(2,1)S(1)}, u32[]{:S(2)}, u32[]{:S(2)}) collective-permute-start(bf16[96,4608]{1,0:T(8,128)(2,1)S(1)} %collective-permute-done.24.mine_ref), channel_id=1, source_target_pairs={{0,4},{1,5},{2,0},{3,1},{4,6},{5,7},{6,2},{7,3},{8,12},{9,13},{10,... | collective-permute-start | bytes 2654216 | tf_op jit(solution)/shard_map/ppermute | solution.py:140
  176.7 42.2 %collective-permute-start.15 = (bf16[192,2304]{1,0:T(8,128)(2,1)S(1)}, bf16[192,2304]{1,0:T(8,128)(2,1)S(1)}, u32[]{:S(2)}, u32[]{:S(2)}) collective-permute-start(bf16[192,2304]{1,0:T(8,128)(2,1)S(1)} %shard_map.117), channel_id=1, source_target_pairs={{0,8},{1,9},{2,10},{3,11},{4,12},{5,13},{6,14},{7,15},{8,0},{9,1},... | collective-permute-start | bytes 2654216 | tf_op jit(solution)/shard_map/ppermute | solution.py:140
  177.9 41.0 %collective-permute-start.18 = (bf16[192,2304]{1,0:T(8,128)(2,1)S(1)}, bf16[192,2304]{1,0:T(8,128)(2,1)S(1)}, u32[]{:S(2)}, u32[]{:S(2)}) collective-permute-start(bf16[192,2304]{1,0:T(8,128)(2,1)S(1)} %shard_map.118), channel_id=1, source_target_pairs={{0,16},{1,17},{2,18},{3,19},{4,20},{5,21},{6,22},{7,23},{8,24},{9,... | collective-permute-start | bytes 2654216 | tf_op jit(solution)/shard_map/ppermute | solution.py:140
  218.9 48.6 %collective-permute-start.27 = (bf16[96,4608]{1,0:T(8,128)(2,1)S(1)}, bf16[96,4608]{1,0:T(8,128)(2,1)S(1)}, u32[]{:S(2)}, u32[]{:S(2)}) collective-permute-start(bf16[96,4608]{1,0:T(8,128)(2,1)S(1)} %collective-permute-done.26.mine_ref), channel_id=1, source_target_pairs={{0,1},{1,0},{2,3},{3,2},{4,5},{5,4},{6,7},{7,6},{8,9},{9,8},{10,11... | collective-permute-start | bytes 2654216 | tf_op jit(solution)/shard_map/ppermute | solution.py:140
  218.9 60.0 %collective-permute-start.42 = (bf16[96,4608]{1,0:T(8,128)(2,1)S(1)}, bf16[96,4608]{1,0:T(8,128)(2,1)S(1)}, u32[]{:S(2)}, u32[]{:S(2)}) collective-permute-start(bf16[96,4608]{1,0:T(8,128)(2,1)S(1)} %collective-permute-done.29.mine_ref), channel_id=1, source_target_pairs={{0,4},{1,5},{2,0},{3,1},{4,6},{5,7},{6,2},{7,3},{8,12},{9,13},{10,... | collective-permute-start | bytes 2654216 | tf_op jit(solution)/shard_map/ppermute | solution.py:140
  236.1 44.2 %collective-permute-start.30 = (bf16[96,4608]{1,0:T(8,128)(2,1)S(1)}, bf16[96,4608]{1,0:T(8,128)(2,1)S(1)}, u32[]{:S(2)}, u32[]{:S(2)}) collective-permute-start(bf16[96,4608]{1,0:T(8,128)(2,1)S(1)} %collective-permute-done.29.mine_ref), channel_id=1, source_target_pairs={{0,1},{1,0},{2,3},{3,2},{4,5},{5,4},{6,7},{7,6},{8,9},{9,8},{10,11... | collective-permute-start | bytes 2654216 | tf_op jit(solution)/shard_map/ppermute | solution.py:140
  278.9 60.6 %collective-permute-start.28 = (bf16[192,2304]{1,0:T(8,128)(2,1)S(1)}, bf16[192,2304]{1,0:T(8,128)(2,1)S(1)}, u32[]{:S(2)}, u32[]{:S(2)}) collective-permute-start(bf16[192,2304]{1,0:T(8,128)(2,1)S(1)} %shard_map.121), channel_id=1, source_target_pairs={{0,8},{1,9},{2,10},{3,11},{4,12},{5,13},{6,14},{7,15},{8,0},{9,1},... | collective-permute-start | bytes 2654216 | tf_op jit(solution)/shard_map/ppermute | solution.py:140
  292.6 48.3 %collective-permute-start.31 = (bf16[192,2304]{1,0:T(8,128)(2,1)S(1)}, bf16[192,2304]{1,0:T(8,128)(2,1)S(1)}, u32[]{:S(2)}, u32[]{:S(2)}) collective-permute-start(bf16[192,2304]{1,0:T(8,128)(2,1)S(1)} %shard_map.122), channel_id=1, source_target_pairs={{0,16},{1,17},{2,18},{3,19},{4,20},{5,21},{6,22},{7,23},{8,24},{9,... | collective-permute-start | bytes 2654216 | tf_op jit(solution)/shard_map/ppermute | solution.py:140
  316.8 71.3 %collective-permute-start.10 = (f32[96,2304]{1,0:T(8,128)S(1)}, f32[96,2304]{1,0:T(8,128)S(1)}, u32[]{:S(2)}, u32[]{:S(2)}) collective-permute-start(f32[96,2304]{1,0:T(8,128)S(1)} %slice.41), channel_id=1, source_target_pairs={{0,1},{1,0},{2,3},{3,2},{4,5},{5,4},{6,7},{7,6},{8,9},{9,8},{10,11... | collective-permute-start | bytes 2654216 | tf_op jit(solution)/shard_map/ppermute | solution.py:140
  328.1 79.2 %collective-permute-start.22 = (bf16[96,2304]{1,0:T(8,128)(2,1)S(1)}, bf16[96,2304]{1,0:T(8,128)(2,1)}, u32[]{:S(2)}, u32[]{:S(2)}) collective-permute-start(bf16[96,2304]{1,0:T(8,128)(2,1)S(1)} %get-tuple-element.33), channel_id=1, source_target_pairs={{0,2},{1,3},{2,6},{3,7},{4,0},{5,1},{6,4},{7,5},{8,10},{9,11},{10,... | collective-permute-start | bytes 1327112 | tf_op jit(solution)/shard_map/ppermute | solution.py:140
  341.0 40.2 %collective-permute-start.44 = (bf16[192,2304]{1,0:T(8,128)(2,1)S(1)}, bf16[192,2304]{1,0:T(8,128)(2,1)S(1)}, u32[]{:S(2)}, u32[]{:S(2)}) collective-permute-start(bf16[192,2304]{1,0:T(8,128)(2,1)S(1)} %shard_map.126), channel_id=1, source_target_pairs={{0,16},{1,17},{2,18},{3,19},{4,20},{5,21},{6,22},{7,23},{8,24},{9,... | collective-permute-start | bytes 2654216 | tf_op jit(solution)/shard_map/ppermute | solution.py:140
  362.1 45.2 %collective-permute-start.23 = (bf16[96,2304]{1,0:T(8,128)(2,1)S(1)}, bf16[96,2304]{1,0:T(8,128)(2,1)}, u32[]{:S(2)}, u32[]{:S(2)}) collective-permute-start(bf16[96,2304]{1,0:T(8,128)(2,1)S(1)} %get-tuple-element.34), channel_id=1, source_target_pairs={{0,3},{1,2},{2,7},{3,6},{4,1},{5,0},{6,5},{7,4},{8,11},{9,10},{10,... | collective-permute-start | bytes 1327112 | tf_op jit(solution)/shard_map/ppermute | solution.py:140
  (52 other events, 1150.9 us)

commit v2 on v0

--- a/solution.py
+++ b/solution.py
@@ -1,14 +1,485 @@
+import functools
+
 import jax
 import jax.numpy as jnp
 from jax import lax
+from jax.experimental import pallas as pl
+from jax.experimental.pallas import tpu as pltpu
 from jax.sharding import PartitionSpec as P
 
 O = 48
 V = 384
 NVEC = 64
-
-
-def on_device(
+CORES = 2
+AXES = ("row", "col")
+POWER = 16
+FLOOR = 2.0**-7.75
+PART_GAIN = 16.0
+SUM_GAIN = 8.0
+
+
+def encode(value, gain):
+    size = jnp.abs(value) * gain + FLOOR
+    size = size * size
+    size = size * size
+    size = size * size
+    size = size * size
+    return jnp.where(value < 0, -size, size).astype(jnp.bfloat16)
+
+
+def decode(code, gain):
+    wide = code.astype(jnp.float32)
+    size = (jnp.exp2(jnp.log2(jnp.abs(wide)) * (1.0 / POWER)) - FLOOR) * (1.0 / gain)
+    return jnp.where(wide < 0, -size, size)
+
+
+def product_kernel(coded, *refs):
+    count = len(coded)
+    parts = refs[:count]
+    own_ref, other_ref, ladder_ref = refs[count : count + 3]
+    outs = refs[count + 3 : 2 * count + 3]
+    rows_buf, cycle_buf, ladder_buf, sems, row_sems = refs[2 * count + 3 :]
+    local_rows, depth = parts[0].shape
+    slots, _, width = cycle_buf.shape
+    blocks = own_ref.shape[1] // width
+    q_part = depth // V
+    j_part = ladder_ref.shape[0] // O
+
+    def cycle_copy(half, b):
+        at = pl.multiple_of(b * width, width)
+        slot = lax.rem(half * blocks + b, slots)
+        return pltpu.make_async_copy(
+            (other_ref if half else own_ref).at[:, pl.ds(at, width)],
+            cycle_buf.at[slot],
+            sems.at[slot],
+        )
+
+    def start(b):
+        @pl.when(b < blocks)
+        def _():
+            cycle_copy(0, b).start()
+
+        @pl.when((b >= blocks) & (b < CORES * blocks))
+        def _():
+            cycle_copy(1, b - blocks).start()
+
+    copies = [
+        pltpu.make_async_copy(part, rows_buf.at[pl.ds(k * local_rows, local_rows)], row_sems.at[k])
+        for k, part in enumerate(parts)
+    ]
+    for copy in copies:
+        copy.start()
+    for b in range(slots - 1):
+        start(jnp.int32(b))
+    for copy in copies:
+        copy.wait()
+    for n in range(count * local_rows // O):
+        stacked = jnp.concatenate(
+            [rows_buf[n * O : (n + 1) * O, q * V : (q + 1) * V] for q in range(q_part)], axis=0
+        )
+        term = jnp.dot(ladder_ref[...], stacked, preferred_element_type=jnp.float32)
+        for j in range(j_part):
+            ladder_buf[n * O : (n + 1) * O, j * V : (j + 1) * V] = term[j * O : (j + 1) * O]
+
+    @pl.loop(0, CORES * blocks)
+    def _(b):
+        start(b + slots - 1)
+        slot = lax.rem(b, slots)
+        pltpu.make_async_copy(
+            own_ref.at[:, pl.ds(0, width)], cycle_buf.at[slot], sems.at[slot]
+        ).wait()
+        columns = pl.ds(pl.multiple_of(b * width, width), width)
+        value = jnp.dot(rows_buf[...], cycle_buf[slot], preferred_element_type=jnp.float32)
+        value = value + ladder_buf[:, columns]
+        for k in range(count):
+            piece = value[k * local_rows : (k + 1) * local_rows]
+            outs[k][:, columns] = encode(piece, PART_GAIN) if coded[k] else piece
+
+
+def product(parts, cycle_block, other_block, ladder_rows, coded):
+    local_rows, depth = parts[0].shape
+    out_width = CORES * cycle_block.shape[1]
+    width = 256 if cycle_block.shape[1] % 256 == 0 else V
+    count = len(parts)
+    rows = count * local_rows
+    slots = 6
+    hbm = pl.BlockSpec(memory_space=pl.ANY)
+    vmem = pl.BlockSpec(memory_space=pltpu.VMEM)
+    return pl.pallas_call(
+        functools.partial(product_kernel, coded),
+        in_specs=[hbm] * (count + 2) + [vmem],
+        out_specs=[vmem] * count,
+        out_shape=[
+            jax.ShapeDtypeStruct((local_rows, out_width), jnp.bfloat16 if c else jnp.float32)
+            for c in coded
+        ],
+        scratch_shapes=[
+            pltpu.VMEM((rows, depth), jnp.bfloat16),
+            pltpu.VMEM((slots, depth, width), jnp.bfloat16),
+            pltpu.VMEM((rows, out_width), jnp.float32),
+            pltpu.SemaphoreType.DMA((slots,)),
+            pltpu.SemaphoreType.DMA((count,)),
+        ],
+        compiler_params=pltpu.CompilerParams(vmem_limit_bytes=48 * 1024 * 1024),
+        cost_estimate=pl.CostEstimate(
+            flops=2 * rows * out_width, bytes_accessed=2 * rows * out_width, transcendentals=0
+        ),
+    )(*parts, cycle_block, other_block, ladder_rows)
+
+
+def power_of_two(exponent):
+    return jnp.exp2(exponent).astype(jnp.bfloat16)
+
+
+def after(value, *earlier):
+    return lax.optimization_barrier((value,) + earlier)[0]
+
+
+SUMS = 5
+
+
+def sums_kernel(blocks, last, starts, occ, grow, rr, beta_prev, vir_ref, acc_in, r_ref, prev_ref, *refs):
+    refs = refs[1:] if last else refs
+    codes = refs[: blocks // CORES]
+    sigma_ref, acc_ref, code_buf, r_buf, prev_buf, sigma_buf, sems = refs[blocks // CORES :]
+    local_rows, row_width = r_ref.shape
+    out_width = codes[0].shape[1] // CORES
+    vectors = local_rows // O
+    count_all = float(O * O * V)
+    copies = []
+    outward = []
+    for b in range(blocks):
+        columns = pl.ds(pl.multiple_of(starts[b], out_width), out_width)
+        copies.append(
+            [
+                pltpu.make_async_copy(
+                    codes[b // CORES].at[:, pl.ds(b % CORES * out_width, out_width)],
+                    code_buf.at[b],
+                    sems.at[0, b],
+                ),
+                pltpu.make_async_copy(r_ref.at[:, columns], r_buf.at[b], sems.at[1, b]),
+                pltpu.make_async_copy(prev_ref.at[:, columns], prev_buf.at[b], sems.at[2, b]),
+            ]
+        )
+        outward.append(
+            pltpu.make_async_copy(sigma_buf.at[b], sigma_ref.at[:, columns], sems.at[3, b])
+        )
+    for group in copies:
+        for copy in group:
+            copy.start()
+    occ_column = lax.broadcasted_iota(jnp.int32, (O, 1), 0)
+    occ_rows = jnp.zeros((O, 1), jnp.float32)
+    for i in range(O):
+        occ_rows = jnp.where(occ_column == i, occ[i], occ_rows)
+    base = vir_ref[...] - occ_rows
+    acc_ref[...] = acc_in[...]
+
+    def folded(value):
+        return jnp.sum(value.reshape(O // 8, 8, V), axis=0)
+
+    for b in range(blocks):
+        for copy in copies[b]:
+            copy.wait()
+
+        @pl.loop(0, out_width // V)
+        def _(j):
+            columns = pl.ds(pl.multiple_of(j * V, V), V)
+            level = base - occ[starts[b] // V + j]
+            for v in range(vectors):
+                rows = pl.ds(v * O, O)
+                r = r_buf[b, rows, columns].astype(jnp.float32)
+                p = prev_buf[b, rows, columns].astype(jnp.float32)
+                value = decode(code_buf[b, rows, columns], SUM_GAIN) * grow[v] + level * r
+                sigma_buf[b, rows, columns] = value
+                for k, term in enumerate((value * value, value * r, value * p, r * p, p * p)):
+                    acc_ref[SUMS * v + k] += folded(term)
+
+        outward[b].start()
+    if last:
+        for v in range(vectors):
+            ss, rs, sp, rp, pp = [
+                jnp.full((1, 128), jnp.sum(acc_ref[SUMS * v + k])) for k in range(SUMS)
+            ]
+            beta = beta_prev[v]
+            alpha = rs / count_all / (rr[v] / count_all + 1e-06)
+            norm = (
+                ss
+                - 2.0 * alpha * rs
+                - 2.0 * beta * sp
+                + alpha * alpha * rr[v]
+                + 2.0 * alpha * beta * rp
+                + beta * beta * pp
+            )
+            acc_ref[SUMS * v, 0:1, 0:128] = alpha
+            acc_ref[SUMS * v, 1:2, 0:128] = jnp.sqrt(norm / count_all + 1e-06)
+    for copy in outward:
+        copy.wait()
+
+
+def add_sums(codes, starts, last, scalars, vir_row, acc, sigma, r_vector, r_previous):
+    local_rows, row_width = r_vector.shape
+    blocks = CORES * len(codes)
+    out_width = codes[0].shape[1] // CORES
+    smem = pl.BlockSpec(memory_space=pltpu.SMEM)
+    hbm = pl.BlockSpec(memory_space=pl.ANY)
+    vmem = pl.BlockSpec(memory_space=pltpu.VMEM)
+    work = blocks * local_rows * out_width
+    held = [sigma] if last else []
+    return pl.pallas_call(
+        functools.partial(sums_kernel, blocks, last),
+        in_specs=[smem] * 5 + [vmem] * 2 + [hbm] * (2 + len(held) + len(codes)),
+        out_specs=(hbm, vmem),
+        out_shape=(
+            jax.ShapeDtypeStruct((local_rows, row_width), jnp.float32),
+            jax.ShapeDtypeStruct(acc.shape, jnp.float32),
+        ),
+        scratch_shapes=[
+            pltpu.VMEM((blocks, local_rows, out_width), jnp.bfloat16),
+            pltpu.VMEM((blocks, local_rows, out_width), jnp.bfloat16),
+            pltpu.VMEM((blocks, local_rows, out_width), jnp.bfloat16),
+            pltpu.VMEM((blocks, local_rows, out_width), jnp.float32),
+            pltpu.SemaphoreType.DMA((4, blocks)),
+        ],
+        input_output_aliases={9: 0} if last else {},
+        compiler_params=pltpu.CompilerParams(vmem_limit_bytes=58 * 1024 * 1024),
+        cost_estimate=pl.CostEstimate(
+            flops=30 * work, bytes_accessed=10 * work, transcendentals=2 * work
+        ),
+    )(starts, *scalars, vir_row, acc, r_vector, r_previous, *held, *codes)
+
+
+def next_kernel(beta_prev, acc_ref, sigma_ref, r_ref, prev_ref, out_ref):
+    for v in range(r_ref.shape[0] // O):
+        rows = pl.ds(v * O, O)
+        alpha = acc_ref[SUMS * v, 0:1, 0:1]
+        scale = 1.0 / acc_ref[SUMS * v, 1:2, 0:1]
+        value = (
+            sigma_ref[rows, :]
+            - alpha * r_ref[rows, :].astype(jnp.float32)
+            - beta_prev[v] * prev_ref[rows, :].astype(jnp.float32)
+        )
+        out_ref[rows, :] = (value * scale).astype(out_ref.dtype)
+
+
+def next_rows(beta_here, acc, sigma, r_vector, r_previous, width):
+    local_rows, row_width = r_vector.shape
+    block = pl.BlockSpec((local_rows, width), lambda i: (0, i))
+    return pl.pallas_call(
+        next_kernel,
+        grid=(row_width // width,),
+        in_specs=[
+            pl.BlockSpec(memory_space=pltpu.SMEM),
+            pl.BlockSpec(acc.shape, lambda i: (0, 0, 0)),
+            block,
+            block,
+            block,
+        ],
+        out_specs=block,
+        out_shape=jax.ShapeDtypeStruct((local_rows, row_width), jnp.bfloat16),
+        compiler_params=pltpu.CompilerParams(vmem_limit_bytes=58 * 1024 * 1024),
+        cost_estimate=pl.CostEstimate(
+            flops=6 * local_rows * row_width,
+            bytes_accessed=10 * local_rows * row_width,
+            transcendentals=0,
+        ),
+    )(beta_here, acc, sigma, r_vector, r_previous)
+
+
+def streamed(
+    r_vector, r_previous, cycle_block, ladder_block, occ_energy, vir_energy, beta_previous
+):
+    n_row = lax.axis_size("row")
+    n_col = lax.axis_size("col")
+    n_chip = n_col // CORES
+    local_rows, row_width = r_vector.shape
+    vectors = local_rows // O
+    depth = row_width // n_row
+    out_width = cycle_block.shape[1]
+    j_part = ladder_block.shape[1]
+    q_part = ladder_block.shape[3]
+    row_at = lax.axis_index("row")
+    col_at = lax.axis_index("col")
+    chip_at = col_at // CORES
+    core_at = col_at % CORES
+    order = list(range(0, n_chip, 2)) + list(range(1, n_chip, 2))[::-1]
+    place = [order.index(chip) for chip in range(n_chip)]
+    paired = n_row & (n_row - 1) == 0
+
+    def partner(row, m):
+        return row ^ m if paired else (row + m) % n_row
+
+    def back(row, m):
+        return row ^ m if paired else (row + n_row - m) % n_row
+
+    def send(value, rows=0, hops=0, swap=0, reverse=False, route=None):
+        pairs = []
+        for row in range(n_row):
+            for chip in range(n_chip):
+                for core in range(CORES):
+                    to_row = back(row, rows) if reverse else partner(row, rows)
+                    to_chip = route[chip] if route else order[(place[chip] + hops) % n_chip]
+                    to_core = (core + swap) % CORES
+                    pairs.append(
+                        (
+                            row * n_col + chip * CORES + core,
+                            to_row * n_col + to_chip * CORES + to_core,
+                        )
+                    )
+        return lax.ppermute(value, AXES, pairs)
+
+    other_block = send(cycle_block, swap=1)
+    r_float = r_vector.astype(jnp.float32)
+    rr_sum = jnp.sum(r_float.reshape(vectors, O * row_width) ** 2, axis=1)
+    exponent = jnp.clip(jnp.floor(0.5 * jnp.log2(jnp.maximum(rr_sum, 1e-37))), -60.0, 60.0)
+    shrink = jnp.repeat(power_of_two(-exponent), O)
+    grow = power_of_two(exponent).astype(jnp.float32)
+
+    def own_part(m):
+        at = partner(row_at, m) * depth
+        return lax.dynamic_slice_in_dim(r_vector, at, depth, axis=1) * shrink[:, None]
+
+    mine = {(0, 0): own_part(0)}
+    for m in range(1, n_row):
+        part = own_part(m)
+        if m == n_row - 1 and m > 2:
+            part = after(part, mine[0, 1], mine[0, 2])
+        mine[0, m] = send(part, rows=m)
+    ladder_rows = after(ladder_block, mine[0, 1]).transpose(1, 0, 3, 2).reshape(j_part * O, q_part * O)
+    ladder_rows = jnp.concatenate([ladder_rows, send(ladder_rows, swap=1)], axis=0)
+    turns = []
+    for s in range(n_chip):
+        if s < 2:
+            turn = list(range(n_row))
+        else:
+            turn = list(range(1, n_row)) + [0]
+        turns += [(s, m) for m in turn]
+    owner_sends = []
+    for chip in range(n_chip):
+        before = order[(place[chip] + n_chip - 1) % n_chip]
+        owner = order[(place[chip] + 1) % n_chip]
+        owner_sends.append((owner, chip, True) if abs(owner - chip) < abs(before - chip) else (before, chip, False))
+    nearest = n_chip > 2 and len({source for source, _, _ in owner_sends}) == n_chip
+    route = {source: chip for source, chip, _ in owner_sends}
+    as_owner = jnp.array(
+        [own for source in range(n_chip) for at, _, own in owner_sends if at == source][:n_chip]
+        if nearest
+        else [False] * n_chip
+    )[chip_at]
+    def pass_on(g, *earlier):
+        s, m = turns[g]
+        part = mine[s - 1, m]
+        if s == n_chip - 1 and nearest:
+            part = jnp.where(as_owner, mine[0, m], part)
+        if g - 3 >= n_row:
+            earlier += (mine[turns[g - 3]],)
+        if earlier:
+            part = after(part, *earlier)
+        if s == n_chip - 1 and nearest:
+            mine[s, m] = send(part, route=route)
+        else:
+            mine[s, m] = send(part, hops=1)
+
+    order_table = jnp.array(order, dtype=jnp.int32)
+    place_at = jnp.array(place, dtype=jnp.int32)[chip_at]
+    starts = []
+    for s in range(n_chip):
+        for swap in range(CORES):
+            chip = order_table[(place_at + s) % n_chip]
+            starts.append((chip * CORES + (core_at + swap) % CORES) * out_width)
+    starts = jnp.stack(starts)
+    linear_index = row_at * n_col + col_at
+    beta_here = lax.dynamic_slice_in_dim(beta_previous, linear_index * vectors, vectors)
+    scalars = (occ_energy, grow, rr_sum, beta_here)
+
+    groups = []
+    for s in range(n_chip):
+        turn = [(s, m) for m in list(range(1, n_row)) + [0]]
+        if s < n_chip - 1:
+            groups += [turn[k : k + 2] for k in range(0, n_row, 2)]
+        else:
+            groups += [turn[:2]] + [[at] for at in turn[2:]]
+    last_of = {group[0][0]: g for g, group in enumerate(groups)}
+    parts = {}
+    arrived = {}
+    codes = {}
+
+    def summed(s):
+        total = parts[s, 0]
+        for k in range(1, n_row):
+            total = total + decode(arrived[s, k], PART_GAIN)
+        return encode(total, SUM_GAIN)
+
+    sent = n_row
+    while sent < min(2 * n_row, len(turns)):
+        pass_on(sent, *([other_block] if sent == 2 * n_row - 1 else []))
+        sent += 1
+    acc = jnp.zeros((vectors * SUMS, 8, V), jnp.float32)
+    vir_row = vir_energy[None, :]
+    start_early, start_late = starts[: CORES * (n_chip - 1)], starts[CORES * (n_chip - 1) :]
+    for g, group in enumerate(groups):
+        s = group[0][0]
+        earlier = []
+        if g > 0:
+            earlier.append(parts[groups[g - 1][0]])
+        if g > 1:
+            earlier += [arrived[at] for at in groups[g - 2] if at in arrived]
+        for k in range(n_chip - 1):
+            if last_of[k] + (2 if k < n_chip - 2 else 1) == g:
+                code = summed(k)
+                earlier.append(code)
+                codes[k] = send(code, hops=n_chip - k) if k > 0 else code
+        if n_row + g + 1 < sent and 0 < g <= n_row:
+            earlier.append(mine[turns[n_row + g + 1]])
+        for k in range(1, n_chip - 1):
+            if k in codes and k < n_chip - 2 and g == last_of[k] + 4:
+                earlier.append(codes[k])
+        while any(at not in mine for at in group):
+            pass_on(sent)
+            sent += 1
+        pieces = [mine[at] for at in group]
+        if g == 0:
+            pieces[0], start_early, start_late, vir_row, acc, *scalars = lax.optimization_barrier(
+                (pieces[0], start_early, start_late, vir_row, acc, *scalars)
+            )
+        if earlier:
+            pieces[0] = after(pieces[0], *earlier)
+        made = product(pieces, cycle_block, other_block, ladder_rows, [m != 0 for _, m in group])
+        for at, part in zip(group, made):
+            parts[at] = part
+            if at[1] != 0:
+                arrived[at] = send(part, rows=at[1], reverse=True)
+        if sent < len(turns):
+            pass_on(sent, made[0])
+            sent += 1
+        if sent < len(turns) and g >= len(groups) - n_row - 1:
+            pass_on(sent)
+            sent += 1
+    s = n_chip - 1
+    if n_chip > 2:
+        parts[s, 0] = after(parts[s, 0], codes[n_chip - 2])
+    code = summed(s)
+    codes[s] = send(code, hops=n_chip - s)
+    early = [codes[k] for k in range(n_chip - 1)]
+    late = [codes[s]]
+    early[0] = after(early[0], code)
+    sigma, acc = add_sums(
+        early, start_early, False, scalars, vir_row, acc, None, r_vector, r_previous
+    )
+    sigma, acc = add_sums(
+        late, start_late, True, scalars, vir_row, acc, sigma, r_vector, r_previous
+    )
+    next_vector = next_rows(beta_here, acc, sigma, r_vector, r_previous, out_width)
+    both = acc.reshape(vectors, SUMS, 8, V)[:, 0, :2, 0].T
+    whole = lax.dynamic_update_slice(
+        jnp.zeros((2, NVEC), jnp.float32), both, (0, linear_index * vectors)
+    )
+    whole = whole + send(whole, swap=1)
+    for group in ([{"hops": h} for h in range(1, n_chip)], [{"rows": m} for m in range(1, n_row)]):
+        whole = sum([send(whole, **kind) for kind in group], whole)
+    return (next_vector, whole[0], whole[1])
+
+
+def gathered(
     r_vector, r_previous, cycle_block, ladder_block, occ_energy, vir_energy, beta_previous
 ):
     n_row = lax.axis_size("row")
@@ -70,7 +541,7 @@
             per_vector(jnp.sum(r_float * prev_float, axis=1)),
             per_vector(jnp.sum(prev_float * prev_float, axis=1)),
         ),
-        ("row", "col"),
+        AXES,
     )
     alpha_coef = rs_sum / count_all / (rr_sum / count_all + 1e-06)
     norm_sum = (
@@ -91,10 +562,16 @@
     return (next_vector, alpha_coef, beta_coef)
 
 
+def on_device(r_vector, *others):
+    whole_vectors = r_vector.shape[0] % O == 0 and lax.axis_size("col") % CORES == 0
+    body = streamed if whole_vectors else gathered
+    return body(r_vector, *others)
+
+
 def solution(mesh):
     placed = (
-        P(("row", "col"), None),
-        P(("row", "col"), None),
+        P(AXES, None),
+        P(AXES, None),
         P("row", "col"),
         P(None, "col", None, "row"),
         P(),
@@ -105,6 +582,6 @@
         on_device,
         mesh=mesh,
         in_specs=placed,
-        out_specs=(P(("row", "col"), None), P(), P()),
+        out_specs=(P(AXES, None), P(), P()),
         check_vma=False,
     )

time: 985 us -> 358 us (0.36)
  waiting for transfers between devices: 641 us -> 84.5 us
  Pallas kernels: 0 us -> 163 us
  matrix products: 107 us -> 0 us
  local copies, waits for them, and re-layouts: 118 us -> 13 us
  blocking collectives: 82.7 us -> 0 us
  starting transfers between devices: 5.26 us -> 65.3 us
    unnamed x3 -> x0, waiting for transfers between devices: 246 us -> none
    all_gather x1 -> x0, waiting for transfers between devices: 245 us -> none  [on_device(): gathered = lax.all_gather(shaped, 'col', axis=1, tiled=True)]
    pallas_call x0 -> x12, Pallas kernels: none -> 163 us  [the longest x9 139 us: product(): pl.pallas_call(functools.partial(product_kernel, coded), in_specs=[hbm] *...]
    all_to_all x1 -> x0, waiting for transfers between devices: 150 us -> none  [on_device(): lax.all_to_all(summed, 'col', split_axis=1, concat_axis=3, tiled=True)]
    dot_general x2 -> x0, matrix products: 107 us -> none  [the longest x1 78.7 us: on_device(): jnp.dot(operand, cycle_block, preferred_element_type=jnp.float32)]
    ppermute x0 -> x39, waiting for transfers between devices: none -> 84.5 us  [send(): return lax.ppermute(value, AXES, pairs)]
    ppermute x0 -> x39, starting transfers between devices: none -> 65.3 us  [send(): return lax.ppermute(value, AXES, pairs)]
    another operation x1, local copies, waits for them, and re-layouts: 48 us -> 0.67 us  [streamed(): starts = jnp.stack(starts)]
  transfers between devices with their start and end apart: 3 -> 39, of which waited for: 3 -> 14; matrix products, arithmetic and copies ran while one was open for 1% -> 9% of each run, Pallas kernels for 0% -> 44%
where the time goes in v2:
time: 358 us; the launch traced here: 357 us
  Pallas kernels  163 us (46%)
  waiting for transfers between devices  84.5 us (24%)
  starting transfers between devices  65.3 us (18%)
  other arithmetic  24 us (7%)
  local copies, waits for them, and re-layouts  13 us (4%)
  between operations  7.56 us (2%)
    pallas_call x9, Pallas kernels, product(): pl.pallas_call(functools.partial(product_kernel, coded), in_specs=[hbm] *...  139 us
    ppermute x39, waiting for transfers between devices, send(): return lax.ppermute(value, AXES, pairs)  84.5 us
    ppermute x39, starting transfers between devices, send(): return lax.ppermute(value, AXES, pairs)  65.3 us
    pallas_call x2, Pallas kernels, add_sums(): pl.pallas_call(functools.partial(sums_kernel, blocks, last), in_specs=[sm...  14.1 us
    convert_element_type x4, other arithmetic, encode(): return jnp.where(value < 0, -size, size).astype(jnp.bfloat16)  13.2 us
    pallas_call x1, Pallas kernels, next_rows(): pl.pallas_call(next_kernel, grid=(row_width // width,), in_specs=[pl.Bloc...  9.83 us
  transfers between devices with their start and end apart: 39, of which 14 were waited for; matrix products, arithmetic and copies ran while one was open for 9% of the time, Pallas kernels for 44%

profile of v2, /device:TPU:0, one launch (start us, length us, event | category | flops | bytes accessed | tf_op | source)
XLA Modules:
  0.0 357.0 jit_solution(16768014317288157300)
XLA Ops:
  4.9 3.7 %dynamic-slice_multiply_fusion = (bf16[96,4608]{1,0:T(8,128)(2,1)S(1)}, bf16[96,4608]{1,0:T(8,128)(2,1)S(1)}, bf16[96,4608]{1,0:T(8,128)(2,1)}, bf16[96,4608]{1,0:T(8,128)(2,1)S(1)}) fusion(bf16[96,18432]{1,0:T(8,128)(2,1)} %r_ref.5, s32[]{:T(128)S(6)} %select_n.177, bf16[96]{0:T(256)(128)(2,1)S(1)} %mul.217, s32[]{:T(128)S(6)} %select_n.176, ...), kind=kLoop, calls=%fused_computation.117 | loop fusion | flops 5750784 | bytes 7078096 | tf_op jit(solution)/shard_map/mul | solution.py:339
  15.3 16.2 %collective-permute-done.refs_0_ = bf16[96,4608]{1,0:T(8,128)(2,1)S(1)} collective-permute-done((bf16[96,4608]{1,0:T(8,128)(2,1)S(1)}, bf16[96,4608]{1,0:T(8,128)(2,1)S(1)}, u32[]{:S(2)}, u32[]{:S(2)}) %collective-permute-start) | collective-permute-done | bytes 884768 | tf_op jit(solution)/shard_map/ppermute | solution.py:328
  54.9 14.8 %shard_map.121 = (bf16[96,4608]{1,0:T(8,128)(2,1)S(1)}, bf16[96,4608]{1,0:T(8,128)(2,1)S(1)}) custom-call(bf16[96,4608]{1,0:T(8,128)(2,1)S(1)} %collective-permute-done.refs_0_, bf16[96,4608]{1,0:T(8,128)(2,1)S(1)} %collective-permute-done.1.refs_1_, bf16[4608,2304]{1,0:T(8,128)(2,1)} %refs_1_.3, bf16[4608,2304]{1,0:T(8,128)(2,1)} %collective-permute-done.3.refs_3_.refs_2_, ...), custom_call_target="tpu_custom_call" | custom-call | flops 1769472 | bytes 1769472 | tf_op jit(solution)/shard_map/pallas_call | solution.py:108
  72.1 14.7 %shard_map.122 = (bf16[96,4608]{1,0:T(8,128)(2,1)S(1)}, f32[96,4608]{1,0:T(8,128)S(1)}) custom-call(bf16[96,4608]{1,0:T(8,128)(2,1)S(1)} %collective-permute-done.2.refs_0_, bf16[96,4608]{1,0:T(8,128)(2,1)S(1)} %get-tuple-element.101.refs_1_, bf16[4608,2304]{1,0:T(8,128)(2,1)} %refs_1_.3, bf16[4608,2304]{1,0:T(8,128)(2,1)} %collective-permute-done.3.refs_3_.refs_2_, ...), custom_call_target="tpu_custom_call" | custom-call | flops 1769472 | bytes 1769472 | tf_op jit(solution)/shard_map/pallas_call | solution.py:108
  94.3 18.2 %shard_map.123 = (bf16[96,4608]{1,0:T(8,128)(2,1)S(1)}, bf16[96,4608]{1,0:T(8,128)(2,1)S(1)}) custom-call(bf16[96,4608]{1,0:T(8,128)(2,1)S(1)} %collective-permute-done.11.refs_0_, bf16[96,4608]{1,0:T(8,128)(2,1)} %collective-permute-done.5.refs_1_, bf16[4608,2304]{1,0:T(8,128)(2,1)} %refs_1_.3, bf16[4608,2304]{1,0:T(8,128)(2,1)} %collective-permute-done.3.refs_3_.refs_2_, ...), custom_call_target="tpu_custom_call" | custom-call | flops 1769472 | bytes 1769472 | tf_op jit(solution)/shard_map/pallas_call | solution.py:108
  113.6 3.4 collective-permute-start.19
  117.0 3.6 %fusion.63.refs_0_ = bf16[96,4608]{1,0:T(8,128)(2,1)} fusion(bf16[96,4608]{1,0:T(8,128)(2,1)S(1)} %collective-permute-done.8, bf16[96,4608]{1,0:T(8,128)(2,1)S(1)} %collective-permute-done.7, f32[96,4608]{1,0:T(8,128)S(1)} %get-tuple-element.64, bf16[96,4608]{1,0:T(8,128)(2,1)S(1)} %collective-permute-done.6), kind=kLoop, calls=%fused_computation.104 | loop fusion | flops 16809984 | bytes 5308416 | tf_op jit(solution)/shard_map/convert_element_type | solution.py:27
  121.2 17.7 %shard_map.124 = (bf16[96,4608]{1,0:T(8,128)(2,1)S(1)}, f32[96,4608]{1,0:T(8,128)S(1)}) custom-call(bf16[96,4608]{1,0:T(8,128)(2,1)S(1)} %collective-permute-done.10.refs_0_, bf16[96,4608]{1,0:T(8,128)(2,1)} %collective-permute-done.9.refs_1_, bf16[4608,2304]{1,0:T(8,128)(2,1)} %refs_1_.3, bf16[4608,2304]{1,0:T(8,128)(2,1)} %collective-permute-done.3.refs_3_.refs_2_, ...), custom_call_target="tpu_custom_call" | custom-call | flops 1769472 | bytes 1769472 | tf_op jit(solution)/shard_map/pallas_call | solution.py:108
  143.8 14.8 %shard_map.125 = (bf16[96,4608]{1,0:T(8,128)(2,1)S(1)}, bf16[96,4608]{1,0:T(8,128)(2,1)S(1)}) custom-call(bf16[96,4608]{1,0:T(8,128)(2,1)S(1)} %collective-permute-done.12.refs_0_, bf16[96,4608]{1,0:T(8,128)(2,1)S(1)} %collective-permute-done.16.refs_1_, bf16[4608,2304]{1,0:T(8,128)(2,1)} %refs_1_.3, ...), custom_call_target="tpu_custom_call" | custom-call | flops 1769472 | bytes 1769472 | tf_op jit(solution)/shard_map/pallas_call | solution.py:108
  161.6 3.9 %fusion.67 = bf16[96,4608]{1,0:T(8,128)(2,1)S(1)} fusion(bf16[96,4608]{1,0:T(8,128)(2,1)} %collective-permute-done.20, bf16[96,4608]{1,0:T(8,128)(2,1)S(1)} %collective-permute-done.15, f32[96,4608]{1,0:T(8,128)S(1)} %get-tuple-element.81, bf16[96,4608]{1,0:T(8,128)(2,1)S(1)} %collective-permute-done.14), kind=kLoop, calls=%fused_computation.108 | loop fusion | flops 16809984 | bytes 5308416 | tf_op jit(solution)/shard_map/convert_element_type | solution.py:27
  165.5 12.5 %collective-permute-start.26 = (bf16[96,4608]{1,0:T(8,128)(2,1)S(1)}, bf16[96,4608]{1,0:T(8,128)(2,1)S(1)}, u32[]{:S(2)}, u32[]{:S(2)}) collective-permute-start(bf16[96,4608]{1,0:T(8,128)(2,1)S(1)} %fusion.67), channel_id=1, source_target_pairs={{0,2},{1,3},{2,6},{3,7},{4,0},{5,1},{6,4},{7,5},{8,10},{9,11},{10,... | collective-permute-start | bytes 2654216 | tf_op jit(solution)/shard_map/ppermute | solution.py:328
  178.0 14.7 %shard_map.126 = (bf16[96,4608]{1,0:T(8,128)(2,1)S(1)}, f32[96,4608]{1,0:T(8,128)S(1)}) custom-call(bf16[96,4608]{1,0:T(8,128)(2,1)S(1)} %collective-permute-done.19.refs_0_, bf16[96,4608]{1,0:T(8,128)(2,1)S(1)} %collective-permute-done.13.refs_1_, bf16[4608,2304]{1,0:T(8,128)(2,1)} %refs_1_.3, bf16[4608,2304]{1,0:T(8,128)(2,1)} %collective-permute-done.3.refs_3_.refs_2_, ...), custom_call_target="tpu_custom_call" | custom-call | flops 1769472 | bytes 1769472 | tf_op jit(solution)/shard_map/pallas_call | solution.py:108
  193.6 3.0 collective-permute-start.23
  199.4 25.4 %collective-permute-done.23 = bf16[96,4608]{1,0:T(8,128)(2,1)S(1)} collective-permute-done((bf16[96,4608]{1,0:T(8,128)(2,1)S(1)}, bf16[96,4608]{1,0:T(8,128)(2,1)S(1)}, u32[]{:S(2)}, u32[]{:S(2)}) %collective-permute-start.23) | collective-permute-done | bytes 884768 | tf_op jit(solution)/shard_map/ppermute | solution.py:328
  229.5 17.2 %collective-permute-done.25.refs_1_ = bf16[96,4608]{1,0:T(8,128)(2,1)S(1)} collective-permute-done((bf16[96,4608]{1,0:T(8,128)(2,1)S(1)}, bf16[96,4608]{1,0:T(8,128)(2,1)S(1)}, u32[]{:S(2)}, u32[]{:S(2)}) %collective-permute-start.25) | collective-permute-done | bytes 884768 | tf_op jit(solution)/shard_map/ppermute | solution.py:328
  246.7 14.8 %shard_map.127 = (bf16[96,4608]{1,0:T(8,128)(2,1)S(1)}, bf16[96,4608]{1,0:T(8,128)(2,1)S(1)}) custom-call(bf16[96,4608]{1,0:T(8,128)(2,1)S(1)} %collective-permute-done.17.refs_0_, bf16[96,4608]{1,0:T(8,128)(2,1)S(1)} %collective-permute-done.25.refs_1_, bf16[4608,2304]{1,0:T(8,128)(2,1)} %refs_1_.3, ...), custom_call_target="tpu_custom_call" | custom-call | flops 1769472 | bytes 1769472 | tf_op jit(solution)/shard_map/pallas_call | solution.py:108
  268.0 14.6 %shard_map.128 = bf16[96,4608]{1,0:T(8,128)(2,1)S(1)} custom-call(bf16[96,4608]{1,0:T(8,128)(2,1)S(1)} %collective-permute-done.21.refs_0_, bf16[4608,2304]{1,0:T(8,128)(2,1)} %refs_1_.3, bf16[4608,2304]{1,0:T(8,128)(2,1)} %collective-permute-done.3.refs_3_.refs_2_, bf16[576,576]{1,0:T(8,128)(2,1)S(1)} %constant_dynamic-update-slice_fusion.refs_4_.refs_3_), custom_call_target="tpu_custom_call" | custom-call | flops 884736 | bytes 884736 | tf_op jit(solution)/shard_map/pallas_call | solution.py:108
  284.1 14.4 %shard_map.129 = f32[96,4608]{1,0:T(8,128)S(1)} custom-call(bf16[96,4608]{1,0:T(8,128)(2,1)S(1)} %collective-permute-done.18.refs_0_, bf16[4608,2304]{1,0:T(8,128)(2,1)} %refs_1_.3, bf16[4608,2304]{1,0:T(8,128)(2,1)} %collective-permute-done.3.refs_3_.refs_2_, bf16[576,576]{1,0:T(8,128)(2,1)S(1)} %constant_dynamic-update-slice_fusion.refs_4_.refs_3_), custom_call_target="tpu_custom_call" | custom-call | flops 884736 | bytes 884736 | tf_op jit(solution)/shard_map/pallas_call | solution.py:108
  298.6 5.3 %collective-permute-done.29.refs_2_ = bf16[96,4608]{1,0:T(8,128)(2,1)S(1)} collective-permute-done((bf16[96,4608]{1,0:T(8,128)(2,1)S(1)}, bf16[96,4608]{1,0:T(8,128)(2,1)S(1)}, u32[]{:S(2)}, u32[]{:S(2)}) %collective-permute-start.29) | collective-permute-done | bytes 884768 | tf_op jit(solution)/shard_map/ppermute | solution.py:328
  309.5 8.7 %shard_map.130 = (f32[96,18432]{1,0:T(8,128)}, f32[10,8,384]{2,1,0:T(8,128)}) custom-call(s32[6]{0:T(128)} %stack.35.starts, f32[48]{0:T(128)} %occ.1, f32[2]{0:T(128)} %get-tuple-element.53.grow, f32[2]{0:T(128)} %copy-done.5, f32[2]{0:T(128)} %dynamic_slice.37.beta_prev, f32[1,384]{1,0:T(1,128)} %broadcast_in_dim.13.vir_ref, ...), custom_call_target="tpu_custom_call" | custom-call | flops 39813120 | bytes 13271040 | tf_op jit(solution)/shard_map/pallas_call | solution.py:228
  318.2 8.1 %collective-permute-done.31.refs_1_ = bf16[96,4608]{1,0:T(8,128)(2,1)S(1)} collective-permute-done((bf16[96,4608]{1,0:T(8,128)(2,1)S(1)}, bf16[96,4608]{1,0:T(8,128)(2,1)S(1)}, u32[]{:S(2)}, u32[]{:S(2)}) %collective-permute-start.31) | collective-permute-done | bytes 884768 | tf_op jit(solution)/shard_map/ppermute | solution.py:328
  327.2 5.5 %shard_map.131 = (f32[96,18432]{1,0:T(8,128)}, f32[10,8,384]{2,1,0:T(8,128)}) custom-call(s32[2]{0:T(128)} %pad_add_fusion.starts, f32[48]{0:T(128)} %occ.1, f32[2]{0:T(128)} %get-tuple-element.53.grow, f32[2]{0:T(128)} %copy-done.5, f32[2]{0:T(128)} %dynamic_slice.37.beta_prev, f32[1,384]{1,0:T(1,128)} %broadcast_in_dim.13.vir_ref, ...), custom_call_target="tpu_custom_call", output_to_operand_aliasing={{0}: (9, {})} | custom-call | flops 13271040 | bytes 4423680 | tf_op jit(solution)/shard_map/pallas_call | solution.py:228
  339.6 2.9 collective-permute-done.34
  346.5 9.8 %shard_map.132 = bf16[96,18432]{1,0:T(8,128)(2,1)} custom-call(f32[2]{0:T(128)} %dynamic_slice.37.beta_prev, f32[10,8,384]{2,1,0:T(8,128)} %get-tuple-element.97.acc_ref, f32[96,18432]{1,0:T(8,128)} %get-tuple-element.98.sigma_ref, bf16[96,18432]{1,0:T(8,128)(2,1)} %r_ref.5, bf16[96,18432]{1,0:T(8,128)(2,1)} %prev_ref.5), custom_call_target="tpu_custom_call" | custom-call | flops 10616832 | bytes 17694720 | tf_op jit(solution)/shard_map/pallas_call | solution.py:267
  (121 shorter events, 81.5 us)
Async XLA Ops:
  0.6 54.3 %collective-permute-start.3 = (bf16[4608,2304]{1,0:T(8,128)(2,1)}, bf16[4608,2304]{1,0:T(8,128)(2,1)}, u32[]{:S(2)}, u32[]{:S(2)}) collective-permute-start(bf16[4608,2304]{1,0:T(8,128)(2,1)} %refs_1_.3), channel_id=1, source_target_pairs={{0,1},{1,0},{2,3},{3,2},{4,5},{5,4},{6,7},{7,6},{8,9},{9,8},{10,11... | collective-permute-start | bytes 63701000 | tf_op jit(solution)/shard_map/ppermute | solution.py:328
  8.6 22.8 %collective-permute-start = (bf16[96,4608]{1,0:T(8,128)(2,1)S(1)}, bf16[96,4608]{1,0:T(8,128)(2,1)S(1)}, u32[]{:S(2)}, u32[]{:S(2)}) collective-permute-start(bf16[96,4608]{1,0:T(8,128)(2,1)S(1)} %get-tuple-element.104), channel_id=1, source_target_pairs={{0,8},{1,9},{2,10},{3,11},{4,12},{5,13},{6,14},{7,15},{8,0},{9,1},... | collective-permute-start | bytes 2654216 | tf_op jit(solution)/shard_map/ppermute | solution.py:328
  12.7 57.6 %collective-permute-start.9 = (bf16[96,4608]{1,0:T(8,128)(2,1)S(1)}, bf16[96,4608]{1,0:T(8,128)(2,1)}, u32[]{:S(2)}, u32[]{:S(2)}) collective-permute-start(bf16[96,4608]{1,0:T(8,128)(2,1)S(1)} %get-tuple-element.101.refs_1_), channel_id=1, source_target_pairs={{0,4},{1,5},{2,0},{3,1},{4,6},{5,7},{6,2},{7,3},{8,12},{9,13},{10,... | collective-permute-start | bytes 2654216 | tf_op jit(solution)/shard_map/ppermute | solution.py:328
  32.9 38.9 %collective-permute-start.2 = (bf16[96,4608]{1,0:T(8,128)(2,1)}, bf16[96,4608]{1,0:T(8,128)(2,1)S(1)}, u32[]{:S(2)}, u32[]{:S(2)}) collective-permute-start(bf16[96,4608]{1,0:T(8,128)(2,1)} %get-tuple-element.59), channel_id=1, source_target_pairs={{0,24},{1,25},{2,26},{3,27},{4,28},{5,29},{6,30},{7,31},{8,16},{9,... | collective-permute-start | bytes 2654216 | tf_op jit(solution)/shard_map/ppermute | solution.py:328
  34.4 37.7 %collective-permute-start.5 = (bf16[96,4608]{1,0:T(8,128)(2,1)S(1)}, bf16[96,4608]{1,0:T(8,128)(2,1)}, u32[]{:S(2)}, u32[]{:S(2)}) collective-permute-start(bf16[96,4608]{1,0:T(8,128)(2,1)S(1)} %collective-permute-done.1.refs_1_), channel_id=1, source_target_pairs={{0,4},{1,5},{2,0},{3,1},{4,6},{5,7},{6,2},{7,3},{8,12},{9,13},{10,... | collective-permute-start | bytes 2654216 | tf_op jit(solution)/shard_map/ppermute | solution.py:328
  52.2 36.8 %collective-permute-start.11 = (bf16[96,4608]{1,0:T(8,128)(2,1)S(1)}, bf16[96,4608]{1,0:T(8,128)(2,1)S(1)}, u32[]{:S(2)}, u32[]{:S(2)}) collective-permute-start(bf16[96,4608]{1,0:T(8,128)(2,1)S(1)} %collective-permute-done.refs_0_), channel_id=1, source_target_pairs={{0,4},{1,5},{2,0},{3,1},{4,6},{5,7},{6,2},{7,3},{8,12},{9,13},{10,... | collective-permute-start | bytes 2654216 | tf_op jit(solution)/shard_map/ppermute | solution.py:328
  70.3 22.5 %collective-permute-start.6 = (bf16[96,4608]{1,0:T(8,128)(2,1)S(1)}, bf16[96,4608]{1,0:T(8,128)(2,1)S(1)}, u32[]{:S(2)}, u32[]{:S(2)}) collective-permute-start(bf16[96,4608]{1,0:T(8,128)(2,1)S(1)} %get-tuple-element.62), channel_id=1, source_target_pairs={{0,8},{1,9},{2,10},{3,11},{4,12},{5,13},{6,14},{7,15},{8,0},{9,1},... | collective-permute-start | bytes 2654216 | tf_op jit(solution)/shard_map/ppermute | solution.py:328
  71.8 22.6 %collective-permute-start.10 = (bf16[96,4608]{1,0:T(8,128)(2,1)S(1)}, bf16[96,4608]{1,0:T(8,128)(2,1)S(1)}, u32[]{:S(2)}, u32[]{:S(2)}) collective-permute-start(bf16[96,4608]{1,0:T(8,128)(2,1)S(1)} %collective-permute-done.2.refs_0_), channel_id=1, source_target_pairs={{0,4},{1,5},{2,0},{3,1},{4,6},{5,7},{6,2},{7,3},{8,12},{9,13},{10,... | collective-permute-start | bytes 2654216 | tf_op jit(solution)/shard_map/ppermute | solution.py:328
  86.9 30.2 %collective-permute-start.8 = (bf16[96,4608]{1,0:T(8,128)(2,1)S(1)}, bf16[96,4608]{1,0:T(8,128)(2,1)S(1)}, u32[]{:S(2)}, u32[]{:S(2)}) collective-permute-start(bf16[96,4608]{1,0:T(8,128)(2,1)S(1)} %get-tuple-element.66), channel_id=1, source_target_pairs={{0,24},{1,25},{2,26},{3,27},{4,28},{5,29},{6,30},{7,31},{8,16},{9,... | collective-permute-start | bytes 2654216 | tf_op jit(solution)/shard_map/ppermute | solution.py:328
  89.0 31.6 %collective-permute-start.12 = (bf16[96,4608]{1,0:T(8,128)(2,1)S(1)}, bf16[96,4608]{1,0:T(8,128)(2,1)S(1)}, u32[]{:S(2)}, u32[]{:S(2)}) collective-permute-start(bf16[96,4608]{1,0:T(8,128)(2,1)S(1)} %collective-permute-done.11.refs_0_), channel_id=1, source_target_pairs={{0,4},{1,5},{2,0},{3,1},{4,6},{5,7},{6,2},{7,3},{8,12},{9,13},{10,... | collective-permute-start | bytes 2654216 | tf_op jit(solution)/shard_map/ppermute | solution.py:328
  91.6 49.8 %collective-permute-start.16 = (bf16[96,4608]{1,0:T(8,128)(2,1)}, bf16[96,4608]{1,0:T(8,128)(2,1)S(1)}, u32[]{:S(2)}, u32[]{:S(2)}) collective-permute-start(bf16[96,4608]{1,0:T(8,128)(2,1)} %collective-permute-done.5.refs_1_), channel_id=1, source_target_pairs={{0,4},{1,5},{2,0},{3,1},{4,6},{5,7},{6,2},{7,3},{8,12},{9,13},{10,... | collective-permute-start | bytes 2654216 | tf_op jit(solution)/shard_map/ppermute | solution.py:328
  112.6 31.3 %collective-permute-start.14 = (bf16[96,4608]{1,0:T(8,128)(2,1)S(1)}, bf16[96,4608]{1,0:T(8,128)(2,1)S(1)}, u32[]{:S(2)}, u32[]{:S(2)}) collective-permute-start(bf16[96,4608]{1,0:T(8,128)(2,1)S(1)} %get-tuple-element.69), channel_id=1, source_target_pairs={{0,8},{1,9},{2,10},{3,11},{4,12},{5,13},{6,14},{7,15},{8,0},{9,1},... | collective-permute-start | bytes 2654216 | tf_op jit(solution)/shard_map/ppermute | solution.py:328
  113.6 64.3 %collective-permute-start.19 = (bf16[96,4608]{1,0:T(8,128)(2,1)S(1)}, bf16[96,4608]{1,0:T(8,128)(2,1)S(1)}, u32[]{:S(2)}, u32[]{:S(2)}) collective-permute-start(bf16[96,4608]{1,0:T(8,128)(2,1)S(1)} %collective-permute-done.10.refs_0_), channel_id=1, source_target_pairs={{0,4},{1,5},{2,0},{3,1},{4,6},{5,7},{6,2},{7,3},{8,12},{9,13},{10,... | collective-permute-start | bytes 2654216 | tf_op jit(solution)/shard_map/ppermute | solution.py:328
  120.6 23.2 %collective-permute-start.15 = (bf16[96,4608]{1,0:T(8,128)(2,1)S(1)}, bf16[96,4608]{1,0:T(8,128)(2,1)S(1)}, u32[]{:S(2)}, u32[]{:S(2)}) collective-permute-start(bf16[96,4608]{1,0:T(8,128)(2,1)S(1)} %get-tuple-element.74), channel_id=1, source_target_pairs={{0,16},{1,17},{2,18},{3,19},{4,20},{5,21},{6,22},{7,23},{8,24},{9,... | collective-permute-start | bytes 2654216 | tf_op jit(solution)/shard_map/ppermute | solution.py:328
  138.9 22.7 %collective-permute-start.20 = (bf16[96,4608]{1,0:T(8,128)(2,1)S(1)}, bf16[96,4608]{1,0:T(8,128)(2,1)}, u32[]{:S(2)}, u32[]{:S(2)}) collective-permute-start(bf16[96,4608]{1,0:T(8,128)(2,1)S(1)} %get-tuple-element.72), channel_id=1, source_target_pairs={{0,24},{1,25},{2,26},{3,27},{4,28},{5,29},{6,30},{7,31},{8,16},{9,... | collective-permute-start | bytes 2654216 | tf_op jit(solution)/shard_map/ppermute | solution.py:328
  141.3 36.6 %collective-permute-start.13 = (bf16[96,4608]{1,0:T(8,128)(2,1)}, bf16[96,4608]{1,0:T(8,128)(2,1)S(1)}, u32[]{:S(2)}, u32[]{:S(2)}) collective-permute-start(bf16[96,4608]{1,0:T(8,128)(2,1)} %collective-permute-done.9.refs_1_), channel_id=1, source_target_pairs={{0,4},{1,5},{2,0},{3,1},{4,6},{5,7},{6,2},{7,3},{8,12},{9,13},{10,... | collective-permute-start | bytes 2654216 | tf_op jit(solution)/shard_map/ppermute | solution.py:328
  158.6 38.8 %collective-permute-start.22 = (bf16[96,4608]{1,0:T(8,128)(2,1)S(1)}, bf16[96,4608]{1,0:T(8,128)(2,1)S(1)}, u32[]{:S(2)}, u32[]{:S(2)}) collective-permute-start(bf16[96,4608]{1,0:T(8,128)(2,1)S(1)} %get-tuple-element.77), channel_id=1, source_target_pairs={{0,8},{1,9},{2,10},{3,11},{4,12},{5,13},{6,14},{7,15},{8,0},{9,1},... | collective-permute-start | bytes 2654216 | tf_op jit(solution)/shard_map/ppermute | solution.py:328
  165.5 102.5 %collective-permute-start.26 = (bf16[96,4608]{1,0:T(8,128)(2,1)S(1)}, bf16[96,4608]{1,0:T(8,128)(2,1)S(1)}, u32[]{:S(2)}, u32[]{:S(2)}) collective-permute-start(bf16[96,4608]{1,0:T(8,128)(2,1)S(1)} %fusion.67), channel_id=1, source_target_pairs={{0,2},{1,3},{2,6},{3,7},{4,0},{5,1},{6,4},{7,5},{8,10},{9,11},{10,... | collective-permute-start | bytes 2654216 | tf_op jit(solution)/shard_map/ppermute | solution.py:328
  192.7 33.9 %collective-permute-start.24 = (bf16[96,4608]{1,0:T(8,128)(2,1)S(1)}, bf16[96,4608]{1,0:T(8,128)(2,1)S(1)}, u32[]{:S(2)}, u32[]{:S(2)}) collective-permute-start(bf16[96,4608]{1,0:T(8,128)(2,1)S(1)} %get-tuple-element.83), channel_id=1, source_target_pairs={{0,24},{1,25},{2,26},{3,27},{4,28},{5,29},{6,30},{7,31},{8,16},{9,... | collective-permute-start | bytes 2654216 | tf_op jit(solution)/shard_map/ppermute | solution.py:328
  193.5 71.6 %collective-permute-start.21 = (bf16[96,4608]{1,0:T(8,128)(2,1)S(1)}, bf16[96,4608]{1,0:T(8,128)(2,1)S(1)}, u32[]{:S(2)}, u32[]{:S(2)}) collective-permute-start(bf16[96,4608]{1,0:T(8,128)(2,1)S(1)} %broadcast_select_fusion.1), channel_id=1, source_target_pairs={{0,2},{1,3},{2,0},{3,1},{4,6},{5,7},{6,4},{7,5},{8,10},{9,11},{10,... | collective-permute-start | bytes 2654216 | tf_op jit(solution)/shard_map/ppermute | solution.py:328
  193.6 31.2 %collective-permute-start.23 = (bf16[96,4608]{1,0:T(8,128)(2,1)S(1)}, bf16[96,4608]{1,0:T(8,128)(2,1)S(1)}, u32[]{:S(2)}, u32[]{:S(2)}) collective-permute-start(bf16[96,4608]{1,0:T(8,128)(2,1)S(1)} %get-tuple-element.85), channel_id=1, source_target_pairs={{0,16},{1,17},{2,18},{3,19},{4,20},{5,21},{6,22},{7,23},{8,24},{9,... | collective-permute-start | bytes 2654216 | tf_op jit(solution)/shard_map/ppermute | solution.py:328
  197.4 32.1 %collective-permute-start.17 = (bf16[96,4608]{1,0:T(8,128)(2,1)S(1)}, bf16[96,4608]{1,0:T(8,128)(2,1)S(1)}, u32[]{:S(2)}, u32[]{:S(2)}) collective-permute-start(bf16[96,4608]{1,0:T(8,128)(2,1)S(1)} %broadcast_select_fusion.2), channel_id=1, source_target_pairs={{0,2},{1,3},{2,0},{3,1},{4,6},{5,7},{6,4},{7,5},{8,10},{9,11},{10,... | collective-permute-start | bytes 2654216 | tf_op jit(solution)/shard_map/ppermute | solution.py:328
  261.5 22.6 %collective-permute-start.28 = (bf16[96,4608]{1,0:T(8,128)(2,1)S(1)}, bf16[96,4608]{1,0:T(8,128)(2,1)S(1)}, u32[]{:S(2)}, u32[]{:S(2)}) collective-permute-start(bf16[96,4608]{1,0:T(8,128)(2,1)S(1)} %get-tuple-element.91), channel_id=1, source_target_pairs={{0,16},{1,17},{2,18},{3,19},{4,20},{5,21},{6,22},{7,23},{8,24},{9,... | collective-permute-start | bytes 2654216 | tf_op jit(solution)/shard_map/ppermute | solution.py:328
  265.1 38.8 %collective-permute-start.29 = (bf16[96,4608]{1,0:T(8,128)(2,1)S(1)}, bf16[96,4608]{1,0:T(8,128)(2,1)S(1)}, u32[]{:S(2)}, u32[]{:S(2)}) collective-permute-start(bf16[96,4608]{1,0:T(8,128)(2,1)S(1)} %fusion.71), channel_id=1, source_target_pairs={{0,6},{1,7},{2,4},{3,5},{4,2},{5,3},{6,0},{7,1},{8,14},{9,15},{10,... | collective-permute-start | bytes 2654216 | tf_op jit(solution)/shard_map/ppermute | solution.py:328
  (25 other events, 321.6 us)

commit v3 on v2

--- a/solution.py
+++ b/solution.py
@@ -135,13 +135,13 @@
     return lax.optimization_barrier((value,) + earlier)[0]
 
 
-SUMS = 5
+SUMS = 3
 
 
 def sums_kernel(blocks, last, starts, occ, grow, rr, beta_prev, vir_ref, acc_in, r_ref, prev_ref, *refs):
     refs = refs[1:] if last else refs
     codes = refs[: blocks // CORES]
-    sigma_ref, acc_ref, code_buf, r_buf, prev_buf, sigma_buf, sems = refs[blocks // CORES :]
+    rest_ref, acc_ref, code_buf, r_buf, prev_buf, rest_buf, sems = refs[blocks // CORES :]
     local_rows, row_width = r_ref.shape
     out_width = codes[0].shape[1] // CORES
     vectors = local_rows // O
@@ -162,7 +162,7 @@
             ]
         )
         outward.append(
-            pltpu.make_async_copy(sigma_buf.at[b], sigma_ref.at[:, columns], sems.at[3, b])
+            pltpu.make_async_copy(rest_buf.at[b], rest_ref.at[:, columns], sems.at[3, b])
         )
     for group in copies:
         for copy in group:
@@ -190,33 +190,26 @@
                 r = r_buf[b, rows, columns].astype(jnp.float32)
                 p = prev_buf[b, rows, columns].astype(jnp.float32)
                 value = decode(code_buf[b, rows, columns], SUM_GAIN) * grow[v] + level * r
-                sigma_buf[b, rows, columns] = value
-                for k, term in enumerate((value * value, value * r, value * p, r * p, p * p)):
+                rest = value - beta_prev[v] * p
+                rest_buf[b, rows, columns] = rest
+                for k, term in enumerate((rest * rest, value * r, rest * r)):
                     acc_ref[SUMS * v + k] += folded(term)
 
         outward[b].start()
     if last:
         for v in range(vectors):
-            ss, rs, sp, rp, pp = [
+            tt, rs, tr = [
                 jnp.full((1, 128), jnp.sum(acc_ref[SUMS * v + k])) for k in range(SUMS)
             ]
-            beta = beta_prev[v]
             alpha = rs / count_all / (rr[v] / count_all + 1e-06)
-            norm = (
-                ss
-                - 2.0 * alpha * rs
-                - 2.0 * beta * sp
-                + alpha * alpha * rr[v]
-                + 2.0 * alpha * beta * rp
-                + beta * beta * pp
-            )
+            norm = tt - 2.0 * alpha * tr + alpha * alpha * rr[v]
             acc_ref[SUMS * v, 0:1, 0:128] = alpha
             acc_ref[SUMS * v, 1:2, 0:128] = jnp.sqrt(norm / count_all + 1e-06)
     for copy in outward:
         copy.wait()
 
 
-def add_sums(codes, starts, last, scalars, vir_row, acc, sigma, r_vector, r_previous):
+def add_sums(codes, starts, last, scalars, vir_row, acc, rest, r_vector, r_previous):
     local_rows, row_width = r_vector.shape
     blocks = CORES * len(codes)
     out_width = codes[0].shape[1] // CORES
@@ -224,7 +217,7 @@
     hbm = pl.BlockSpec(memory_space=pl.ANY)
     vmem = pl.BlockSpec(memory_space=pltpu.VMEM)
     work = blocks * local_rows * out_width
-    held = [sigma] if last else []
+    held = [rest] if last else []
     return pl.pallas_call(
         functools.partial(sums_kernel, blocks, last),
         in_specs=[smem] * 5 + [vmem] * 2 + [hbm] * (2 + len(held) + len(codes)),
@@ -248,29 +241,23 @@
     )(starts, *scalars, vir_row, acc, r_vector, r_previous, *held, *codes)
 
 
-def next_kernel(beta_prev, acc_ref, sigma_ref, r_ref, prev_ref, out_ref):
+def next_kernel(acc_ref, rest_ref, r_ref, out_ref):
     for v in range(r_ref.shape[0] // O):
         rows = pl.ds(v * O, O)
         alpha = acc_ref[SUMS * v, 0:1, 0:1]
         scale = 1.0 / acc_ref[SUMS * v, 1:2, 0:1]
-        value = (
-            sigma_ref[rows, :]
-            - alpha * r_ref[rows, :].astype(jnp.float32)
-            - beta_prev[v] * prev_ref[rows, :].astype(jnp.float32)
-        )
+        value = rest_ref[rows, :] - alpha * r_ref[rows, :].astype(jnp.float32)
         out_ref[rows, :] = (value * scale).astype(out_ref.dtype)
 
 
-def next_rows(beta_here, acc, sigma, r_vector, r_previous, width):
+def next_rows(acc, rest, r_vector, width):
     local_rows, row_width = r_vector.shape
     block = pl.BlockSpec((local_rows, width), lambda i: (0, i))
     return pl.pallas_call(
         next_kernel,
         grid=(row_width // width,),
         in_specs=[
-            pl.BlockSpec(memory_space=pltpu.SMEM),
             pl.BlockSpec(acc.shape, lambda i: (0, 0, 0)),
-            block,
             block,
             block,
         ],
@@ -279,10 +266,10 @@
         compiler_params=pltpu.CompilerParams(vmem_limit_bytes=58 * 1024 * 1024),
         cost_estimate=pl.CostEstimate(
             flops=6 * local_rows * row_width,
-            bytes_accessed=10 * local_rows * row_width,
+            bytes_accessed=8 * local_rows * row_width,
             transcendentals=0,
         ),
-    )(beta_here, acc, sigma, r_vector, r_previous)
+    )(acc, rest, r_vector)
 
 
 def streamed(
@@ -370,8 +357,9 @@
         part = mine[s - 1, m]
         if s == n_chip - 1 and nearest:
             part = jnp.where(as_owner, mine[0, m], part)
-        if g - 3 >= n_row:
-            earlier += (mine[turns[g - 3]],)
+        lag = 2 if s == n_chip - 1 else 3
+        if g - lag >= n_row:
+            earlier += (mine[turns[g - lag]],)
         if earlier:
             part = after(part, *earlier)
         if s == n_chip - 1 and nearest:
@@ -424,7 +412,7 @@
         if g > 1:
             earlier += [arrived[at] for at in groups[g - 2] if at in arrived]
         for k in range(n_chip - 1):
-            if last_of[k] + (2 if k < n_chip - 2 else 1) == g:
+            if last_of[k] + 2 == g:
                 code = summed(k)
                 earlier.append(code)
                 codes[k] = send(code, hops=n_chip - k) if k > 0 else code
@@ -455,20 +443,18 @@
             pass_on(sent)
             sent += 1
     s = n_chip - 1
-    if n_chip > 2:
-        parts[s, 0] = after(parts[s, 0], codes[n_chip - 2])
     code = summed(s)
-    codes[s] = send(code, hops=n_chip - s)
+    codes[s] = send(after(code, codes[n_chip - 2]), hops=n_chip - s)
     early = [codes[k] for k in range(n_chip - 1)]
     late = [codes[s]]
     early[0] = after(early[0], code)
-    sigma, acc = add_sums(
+    rest, acc = add_sums(
         early, start_early, False, scalars, vir_row, acc, None, r_vector, r_previous
     )
-    sigma, acc = add_sums(
-        late, start_late, True, scalars, vir_row, acc, sigma, r_vector, r_previous
-    )
-    next_vector = next_rows(beta_here, acc, sigma, r_vector, r_previous, out_width)
+    rest, acc = add_sums(
+        late, start_late, True, scalars, vir_row, acc, rest, r_vector, r_previous
+    )
+    next_vector = next_rows(acc, rest, r_vector, out_width)
     both = acc.reshape(vectors, SUMS, 8, V)[:, 0, :2, 0].T
     whole = lax.dynamic_update_slice(
         jnp.zeros((2, NVEC), jnp.float32), both, (0, linear_index * vectors)

time: 358 us -> 354 us (0.989)
  waiting for transfers between devices: 84.5 us -> 76.1 us
  starting transfers between devices: 65.3 us -> 69.9 us
    ppermute x39, waiting for transfers between devices: 84.5 us -> 76.1 us  [send(): return lax.ppermute(value, AXES, pairs)]
    ppermute x39, starting transfers between devices: 65.3 us -> 69.9 us  [send(): return lax.ppermute(value, AXES, pairs)]
  transfers between devices with their start and end apart: 39 -> 39, of which waited for: 14 -> 14; matrix products, arithmetic and copies ran while one was open for 9% -> 10% of each run, Pallas kernels for 44% -> 44%
where the time goes in v3:
time: 354 us; the launch traced here: 353 us
  Pallas kernels  161 us (45%)
  waiting for transfers between devices  76.1 us (21%)
  starting transfers between devices  69.9 us (20%)
  other arithmetic  25.2 us (7%)
  local copies, waits for them, and re-layouts  13 us (4%)
  between operations  7.61 us (2%)
    pallas_call x9, Pallas kernels, product(): pl.pallas_call(functools.partial(product_kernel, coded), in_specs=[hbm] *...  139 us
    ppermute x39, waiting for transfers between devices, send(): return lax.ppermute(value, AXES, pairs)  76.1 us
    ppermute x39, starting transfers between devices, send(): return lax.ppermute(value, AXES, pairs)  69.9 us
    convert_element_type x4, other arithmetic, encode(): return jnp.where(value < 0, -size, size).astype(jnp.bfloat16)  14.4 us
    pallas_call x2, Pallas kernels, add_sums(): pl.pallas_call(functools.partial(sums_kernel, blocks, last), in_specs=[sm...  13.6 us
    pallas_call x1, Pallas kernels, next_rows(): pl.pallas_call(next_kernel, grid=(row_width // width,), in_specs=[pl.Bloc...  8.67 us
  transfers between devices with their start and end apart: 39, of which 14 were waited for; matrix products, arithmetic and copies ran while one was open for 10% of the time, Pallas kernels for 44%

profile of v3, /device:TPU:0, one launch (start us, length us, event | category | flops | bytes accessed | tf_op | source)
XLA Modules:
  0.0 352.9 jit_solution(11546635909740392061)
XLA Ops:
  4.9 3.7 %dynamic-slice_multiply_fusion = (bf16[96,4608]{1,0:T(8,128)(2,1)S(1)}, bf16[96,4608]{1,0:T(8,128)(2,1)S(1)}, bf16[96,4608]{1,0:T(8,128)(2,1)}, bf16[96,4608]{1,0:T(8,128)(2,1)S(1)}) fusion(bf16[96,18432]{1,0:T(8,128)(2,1)} %r_ref.5, s32[]{:T(128)S(6)} %select_n.177, bf16[96]{0:T(256)(128)(2,1)S(1)} %mul.215, s32[]{:T(128)S(6)} %select_n.176, ...), kind=kLoop, calls=%fused_computation.117 | loop fusion | flops 5750784 | bytes 7078096 | tf_op jit(solution)/shard_map/mul | solution.py:326
  15.2 16.2 %collective-permute-done.refs_0_ = bf16[96,4608]{1,0:T(8,128)(2,1)S(1)} collective-permute-done((bf16[96,4608]{1,0:T(8,128)(2,1)S(1)}, bf16[96,4608]{1,0:T(8,128)(2,1)S(1)}, u32[]{:S(2)}, u32[]{:S(2)}) %collective-permute-start) | collective-permute-done | bytes 884768 | tf_op jit(solution)/shard_map/ppermute | solution.py:315
  55.0 14.8 %shard_map.121 = (bf16[96,4608]{1,0:T(8,128)(2,1)S(1)}, bf16[96,4608]{1,0:T(8,128)(2,1)S(1)}) custom-call(bf16[96,4608]{1,0:T(8,128)(2,1)S(1)} %collective-permute-done.refs_0_, bf16[96,4608]{1,0:T(8,128)(2,1)S(1)} %collective-permute-done.1.refs_1_, bf16[4608,2304]{1,0:T(8,128)(2,1)} %refs_1_.3, bf16[4608,2304]{1,0:T(8,128)(2,1)} %collective-permute-done.3.refs_3_.refs_2_, ...), custom_call_target="tpu_custom_call" | custom-call | flops 1769472 | bytes 1769472 | tf_op jit(solution)/shard_map/pallas_call | solution.py:108
  72.2 14.7 %shard_map.122 = (bf16[96,4608]{1,0:T(8,128)(2,1)S(1)}, f32[96,4608]{1,0:T(8,128)S(1)}) custom-call(bf16[96,4608]{1,0:T(8,128)(2,1)S(1)} %collective-permute-done.2.refs_0_, bf16[96,4608]{1,0:T(8,128)(2,1)S(1)} %get-tuple-element.101.refs_1_, bf16[4608,2304]{1,0:T(8,128)(2,1)} %refs_1_.3, bf16[4608,2304]{1,0:T(8,128)(2,1)} %collective-permute-done.3.refs_3_.refs_2_, ...), custom_call_target="tpu_custom_call" | custom-call | flops 1769472 | bytes 1769472 | tf_op jit(solution)/shard_map/pallas_call | solution.py:108
  94.4 18.3 %shard_map.123 = (bf16[96,4608]{1,0:T(8,128)(2,1)S(1)}, bf16[96,4608]{1,0:T(8,128)(2,1)S(1)}) custom-call(bf16[96,4608]{1,0:T(8,128)(2,1)S(1)} %collective-permute-done.11.refs_0_, bf16[96,4608]{1,0:T(8,128)(2,1)} %collective-permute-done.5.refs_1_, bf16[4608,2304]{1,0:T(8,128)(2,1)} %refs_1_.3, bf16[4608,2304]{1,0:T(8,128)(2,1)} %collective-permute-done.3.refs_3_.refs_2_, ...), custom_call_target="tpu_custom_call" | custom-call | flops 1769472 | bytes 1769472 | tf_op jit(solution)/shard_map/pallas_call | solution.py:108
  113.6 3.3 collective-permute-start.17
  116.9 3.6 %fusion.63.refs_0_ = bf16[96,4608]{1,0:T(8,128)(2,1)} fusion(bf16[96,4608]{1,0:T(8,128)(2,1)S(1)} %collective-permute-done.8, bf16[96,4608]{1,0:T(8,128)(2,1)S(1)} %collective-permute-done.7, f32[96,4608]{1,0:T(8,128)S(1)} %get-tuple-element.64, bf16[96,4608]{1,0:T(8,128)(2,1)S(1)} %collective-permute-done.6), kind=kLoop, calls=%fused_computation.104 | loop fusion | flops 16809984 | bytes 5308416 | tf_op jit(solution)/shard_map/convert_element_type | solution.py:27
  121.1 17.7 %shard_map.124 = (bf16[96,4608]{1,0:T(8,128)(2,1)S(1)}, f32[96,4608]{1,0:T(8,128)S(1)}) custom-call(bf16[96,4608]{1,0:T(8,128)(2,1)S(1)} %collective-permute-done.10.refs_0_, bf16[96,4608]{1,0:T(8,128)(2,1)} %collective-permute-done.9.refs_1_, bf16[4608,2304]{1,0:T(8,128)(2,1)} %refs_1_.3, bf16[4608,2304]{1,0:T(8,128)(2,1)} %collective-permute-done.3.refs_3_.refs_2_, ...), custom_call_target="tpu_custom_call" | custom-call | flops 1769472 | bytes 1769472 | tf_op jit(solution)/shard_map/pallas_call | solution.py:108
  143.8 14.8 %shard_map.125 = (bf16[96,4608]{1,0:T(8,128)(2,1)S(1)}, bf16[96,4608]{1,0:T(8,128)(2,1)S(1)}) custom-call(bf16[96,4608]{1,0:T(8,128)(2,1)S(1)} %collective-permute-done.12.refs_0_, bf16[96,4608]{1,0:T(8,128)(2,1)S(1)} %collective-permute-done.14.refs_1_, bf16[4608,2304]{1,0:T(8,128)(2,1)} %refs_1_.3, ...), custom_call_target="tpu_custom_call" | custom-call | flops 1769472 | bytes 1769472 | tf_op jit(solution)/shard_map/pallas_call | solution.py:108
  161.7 4.0 %fusion.67 = bf16[96,4608]{1,0:T(8,128)(2,1)S(1)} fusion(bf16[96,4608]{1,0:T(8,128)(2,1)} %collective-permute-done.20, bf16[96,4608]{1,0:T(8,128)(2,1)} %collective-permute-done.19, f32[96,4608]{1,0:T(8,128)S(1)} %get-tuple-element.81, bf16[96,4608]{1,0:T(8,128)(2,1)S(1)} %collective-permute-done.18), kind=kLoop, calls=%fused_computation.108 | loop fusion | flops 16809984 | bytes 5308416 | tf_op jit(solution)/shard_map/convert_element_type | solution.py:27
  165.7 12.4 %collective-permute-start.21 = (bf16[96,4608]{1,0:T(8,128)(2,1)S(1)}, bf16[96,4608]{1,0:T(8,128)(2,1)S(1)}, u32[]{:S(2)}, u32[]{:S(2)}) collective-permute-start(bf16[96,4608]{1,0:T(8,128)(2,1)S(1)} %broadcast_select_fusion), channel_id=1, source_target_pairs={{0,2},{1,3},{2,0},{3,1},{4,6},{5,7},{6,4},{7,5},{8,10},{9,11},{10,... | collective-permute-start | bytes 2654216 | tf_op jit(solution)/shard_map/ppermute | solution.py:315
  178.3 14.7 %shard_map.126 = (bf16[96,4608]{1,0:T(8,128)(2,1)S(1)}, f32[96,4608]{1,0:T(8,128)S(1)}) custom-call(bf16[96,4608]{1,0:T(8,128)(2,1)S(1)} %collective-permute-done.17.refs_0_, bf16[96,4608]{1,0:T(8,128)(2,1)S(1)} %collective-permute-done.13.refs_1_, bf16[4608,2304]{1,0:T(8,128)(2,1)} %refs_1_.3, bf16[4608,2304]{1,0:T(8,128)(2,1)} %collective-permute-done.3.refs_3_.refs_2_, ...), custom_call_target="tpu_custom_call" | custom-call | flops 1769472 | bytes 1769472 | tf_op jit(solution)/shard_map/pallas_call | solution.py:108
  197.5 10.7 %collective-permute-done.21.refs_0_ = bf16[96,4608]{1,0:T(8,128)(2,1)S(1)} collective-permute-done((bf16[96,4608]{1,0:T(8,128)(2,1)S(1)}, bf16[96,4608]{1,0:T(8,128)(2,1)S(1)}, u32[]{:S(2)}, u32[]{:S(2)}) %collective-permute-start.21) | collective-permute-done | bytes 884768 | tf_op jit(solution)/shard_map/ppermute | solution.py:315
  210.1 25.5 %collective-permute-done.15.refs_1_ = bf16[96,4608]{1,0:T(8,128)(2,1)S(1)} collective-permute-done((bf16[96,4608]{1,0:T(8,128)(2,1)S(1)}, bf16[96,4608]{1,0:T(8,128)(2,1)S(1)}, u32[]{:S(2)}, u32[]{:S(2)}) %collective-permute-start.15) | collective-permute-done | bytes 884768 | tf_op jit(solution)/shard_map/ppermute | solution.py:315
  235.6 14.8 %shard_map.127 = (bf16[96,4608]{1,0:T(8,128)(2,1)S(1)}, bf16[96,4608]{1,0:T(8,128)(2,1)S(1)}) custom-call(bf16[96,4608]{1,0:T(8,128)(2,1)S(1)} %collective-permute-done.21.refs_0_, bf16[96,4608]{1,0:T(8,128)(2,1)S(1)} %collective-permute-done.15.refs_1_, bf16[4608,2304]{1,0:T(8,128)(2,1)} %refs_1_.3, ...), custom_call_target="tpu_custom_call" | custom-call | flops 1769472 | bytes 1769472 | tf_op jit(solution)/shard_map/pallas_call | solution.py:108
  252.1 3.9 %fusion.71 = bf16[96,4608]{1,0:T(8,128)(2,1)S(1)} fusion(bf16[96,4608]{1,0:T(8,128)(2,1)} %collective-permute-done.25, bf16[96,4608]{1,0:T(8,128)(2,1)S(1)} %collective-permute-done.24, f32[96,4608]{1,0:T(8,128)S(1)} %get-tuple-element.89, bf16[96,4608]{1,0:T(8,128)(2,1)S(1)} %collective-permute-done.23), kind=kLoop, calls=%fused_computation.112 | loop fusion | flops 16809984 | bytes 5308416 | tf_op jit(solution)/shard_map/convert_element_type | solution.py:27
  256.0 14.6 %shard_map.128 = bf16[96,4608]{1,0:T(8,128)(2,1)S(1)} custom-call(bf16[96,4608]{1,0:T(8,128)(2,1)S(1)} %collective-permute-done.22.refs_0_, bf16[4608,2304]{1,0:T(8,128)(2,1)} %refs_1_.3, bf16[4608,2304]{1,0:T(8,128)(2,1)} %collective-permute-done.3.refs_3_.refs_2_, bf16[576,576]{1,0:T(8,128)(2,1)S(1)} %constant_dynamic-update-slice_fusion.refs_4_.refs_3_), custom_call_target="tpu_custom_call" | custom-call | flops 884736 | bytes 884736 | tf_op jit(solution)/shard_map/pallas_call | solution.py:108
  272.5 14.4 %shard_map.129 = f32[96,4608]{1,0:T(8,128)S(1)} custom-call(bf16[96,4608]{1,0:T(8,128)(2,1)S(1)} %collective-permute-done.16.refs_0_, bf16[4608,2304]{1,0:T(8,128)(2,1)} %refs_1_.3, bf16[4608,2304]{1,0:T(8,128)(2,1)} %collective-permute-done.3.refs_3_.refs_2_, bf16[576,576]{1,0:T(8,128)(2,1)S(1)} %constant_dynamic-update-slice_fusion.refs_4_.refs_3_), custom_call_target="tpu_custom_call" | custom-call | flops 884736 | bytes 884736 | tf_op jit(solution)/shard_map/pallas_call | solution.py:108
  289.9 14.7 %collective-permute-start.31 = (bf16[96,4608]{1,0:T(8,128)(2,1)S(1)}, bf16[96,4608]{1,0:T(8,128)(2,1)S(1)}, u32[]{:S(2)}, u32[]{:S(2)}) collective-permute-start(bf16[96,4608]{1,0:T(8,128)(2,1)S(1)} %fusion.75), channel_id=1, source_target_pairs={{0,4},{1,5},{2,0},{3,1},{4,6},{5,7},{6,2},{7,3},{8,12},{9,13},{10,... | collective-permute-start | bytes 2654216 | tf_op jit(solution)/shard_map/ppermute | solution.py:315
  305.3 8.3 %shard_map.130 = (f32[96,18432]{1,0:T(8,128)}, f32[6,8,384]{2,1,0:T(8,128)}) custom-call(s32[6]{0:T(128)} %stack.35.starts, f32[48]{0:T(128)} %occ.1, f32[2]{0:T(128)} %get-tuple-element.53.grow, f32[2]{0:T(128)} %copy-done.5, f32[2]{0:T(128)} %dynamic_slice.43.beta_prev, f32[1,384]{1,0:T(1,128)} %broadcast_in_dim.13.vir_ref, ...), custom_call_target="tpu_custom_call" | custom-call | flops 39813120 | bytes 13271040 | tf_op jit(solution)/shard_map/pallas_call | solution.py:221
  313.6 9.3 %collective-permute-done.31.refs_1_ = bf16[96,4608]{1,0:T(8,128)(2,1)S(1)} collective-permute-done((bf16[96,4608]{1,0:T(8,128)(2,1)S(1)}, bf16[96,4608]{1,0:T(8,128)(2,1)S(1)}, u32[]{:S(2)}, u32[]{:S(2)}) %collective-permute-start.31) | collective-permute-done | bytes 884768 | tf_op jit(solution)/shard_map/ppermute | solution.py:315
  323.8 5.3 %shard_map.131 = (f32[96,18432]{1,0:T(8,128)}, f32[6,8,384]{2,1,0:T(8,128)}) custom-call(s32[2]{0:T(128)} %pad_add_fusion.starts, f32[48]{0:T(128)} %occ.1, f32[2]{0:T(128)} %get-tuple-element.53.grow, f32[2]{0:T(128)} %copy-done.5, f32[2]{0:T(128)} %dynamic_slice.43.beta_prev, f32[1,384]{1,0:T(1,128)} %broadcast_in_dim.13.vir_ref, ...), custom_call_target="tpu_custom_call", output_to_operand_aliasing={{0}: (9, {})} | custom-call | flops 13271040 | bytes 4423680 | tf_op jit(solution)/shard_map/pallas_call | solution.py:221
  332.7 3.4 collective-permute-start.34
  343.5 8.7 %shard_map.132 = bf16[96,18432]{1,0:T(8,128)(2,1)} custom-call(f32[6,8,384]{2,1,0:T(8,128)} %get-tuple-element.97.acc_ref, f32[96,18432]{1,0:T(8,128)} %get-tuple-element.98.rest_ref, bf16[96,18432]{1,0:T(8,128)(2,1)} %r_ref.5), custom_call_target="tpu_custom_call" | custom-call | flops 10616832 | bytes 14155776 | tf_op jit(solution)/shard_map/pallas_call | solution.py:256
  (121 shorter events, 73.5 us)
Async XLA Ops:
  0.6 54.3 %collective-permute-start.3 = (bf16[4608,2304]{1,0:T(8,128)(2,1)}, bf16[4608,2304]{1,0:T(8,128)(2,1)}, u32[]{:S(2)}, u32[]{:S(2)}) collective-permute-start(bf16[4608,2304]{1,0:T(8,128)(2,1)} %refs_1_.3), channel_id=1, source_target_pairs={{0,1},{1,0},{2,3},{3,2},{4,5},{5,4},{6,7},{7,6},{8,9},{9,8},{10,11... | collective-permute-start | bytes 63701000 | tf_op jit(solution)/shard_map/ppermute | solution.py:315
  8.6 22.8 %collective-permute-start = (bf16[96,4608]{1,0:T(8,128)(2,1)S(1)}, bf16[96,4608]{1,0:T(8,128)(2,1)S(1)}, u32[]{:S(2)}, u32[]{:S(2)}) collective-permute-start(bf16[96,4608]{1,0:T(8,128)(2,1)S(1)} %get-tuple-element.104), channel_id=1, source_target_pairs={{0,8},{1,9},{2,10},{3,11},{4,12},{5,13},{6,14},{7,15},{8,0},{9,1},... | collective-permute-start | bytes 2654216 | tf_op jit(solution)/shard_map/ppermute | solution.py:315
  12.6 57.7 %collective-permute-start.9 = (bf16[96,4608]{1,0:T(8,128)(2,1)S(1)}, bf16[96,4608]{1,0:T(8,128)(2,1)}, u32[]{:S(2)}, u32[]{:S(2)}) collective-permute-start(bf16[96,4608]{1,0:T(8,128)(2,1)S(1)} %get-tuple-element.101.refs_1_), channel_id=1, source_target_pairs={{0,4},{1,5},{2,0},{3,1},{4,6},{5,7},{6,2},{7,3},{8,12},{9,13},{10,... | collective-permute-start | bytes 2654216 | tf_op jit(solution)/shard_map/ppermute | solution.py:315
  32.9 39.0 %collective-permute-start.2 = (bf16[96,4608]{1,0:T(8,128)(2,1)}, bf16[96,4608]{1,0:T(8,128)(2,1)S(1)}, u32[]{:S(2)}, u32[]{:S(2)}) collective-permute-start(bf16[96,4608]{1,0:T(8,128)(2,1)} %get-tuple-element.59), channel_id=1, source_target_pairs={{0,24},{1,25},{2,26},{3,27},{4,28},{5,29},{6,30},{7,31},{8,16},{9,... | collective-permute-start | bytes 2654216 | tf_op jit(solution)/shard_map/ppermute | solution.py:315
  34.4 37.8 %collective-permute-start.5 = (bf16[96,4608]{1,0:T(8,128)(2,1)S(1)}, bf16[96,4608]{1,0:T(8,128)(2,1)}, u32[]{:S(2)}, u32[]{:S(2)}) collective-permute-start(bf16[96,4608]{1,0:T(8,128)(2,1)S(1)} %collective-permute-done.1.refs_1_), channel_id=1, source_target_pairs={{0,4},{1,5},{2,0},{3,1},{4,6},{5,7},{6,2},{7,3},{8,12},{9,13},{10,... | collective-permute-start | bytes 2654216 | tf_op jit(solution)/shard_map/ppermute | solution.py:315
  52.3 36.8 %collective-permute-start.11 = (bf16[96,4608]{1,0:T(8,128)(2,1)S(1)}, bf16[96,4608]{1,0:T(8,128)(2,1)S(1)}, u32[]{:S(2)}, u32[]{:S(2)}) collective-permute-start(bf16[96,4608]{1,0:T(8,128)(2,1)S(1)} %collective-permute-done.refs_0_), channel_id=1, source_target_pairs={{0,4},{1,5},{2,0},{3,1},{4,6},{5,7},{6,2},{7,3},{8,12},{9,13},{10,... | collective-permute-start | bytes 2654216 | tf_op jit(solution)/shard_map/ppermute | solution.py:315
  70.3 22.5 %collective-permute-start.6 = (bf16[96,4608]{1,0:T(8,128)(2,1)S(1)}, bf16[96,4608]{1,0:T(8,128)(2,1)S(1)}, u32[]{:S(2)}, u32[]{:S(2)}) collective-permute-start(bf16[96,4608]{1,0:T(8,128)(2,1)S(1)} %get-tuple-element.62), channel_id=1, source_target_pairs={{0,8},{1,9},{2,10},{3,11},{4,12},{5,13},{6,14},{7,15},{8,0},{9,1},... | collective-permute-start | bytes 2654216 | tf_op jit(solution)/shard_map/ppermute | solution.py:315
  71.8 22.6 %collective-permute-start.10 = (bf16[96,4608]{1,0:T(8,128)(2,1)S(1)}, bf16[96,4608]{1,0:T(8,128)(2,1)S(1)}, u32[]{:S(2)}, u32[]{:S(2)}) collective-permute-start(bf16[96,4608]{1,0:T(8,128)(2,1)S(1)} %collective-permute-done.2.refs_0_), channel_id=1, source_target_pairs={{0,4},{1,5},{2,0},{3,1},{4,6},{5,7},{6,2},{7,3},{8,12},{9,13},{10,... | collective-permute-start | bytes 2654216 | tf_op jit(solution)/shard_map/ppermute | solution.py:315
  86.9 30.0 %collective-permute-start.8 = (bf16[96,4608]{1,0:T(8,128)(2,1)S(1)}, bf16[96,4608]{1,0:T(8,128)(2,1)S(1)}, u32[]{:S(2)}, u32[]{:S(2)}) collective-permute-start(bf16[96,4608]{1,0:T(8,128)(2,1)S(1)} %get-tuple-element.66), channel_id=1, source_target_pairs={{0,24},{1,25},{2,26},{3,27},{4,28},{5,29},{6,30},{7,31},{8,16},{9,... | collective-permute-start | bytes 2654216 | tf_op jit(solution)/shard_map/ppermute | solution.py:315
  89.1 31.5 %collective-permute-start.12 = (bf16[96,4608]{1,0:T(8,128)(2,1)S(1)}, bf16[96,4608]{1,0:T(8,128)(2,1)S(1)}, u32[]{:S(2)}, u32[]{:S(2)}) collective-permute-start(bf16[96,4608]{1,0:T(8,128)(2,1)S(1)} %collective-permute-done.11.refs_0_), channel_id=1, source_target_pairs={{0,4},{1,5},{2,0},{3,1},{4,6},{5,7},{6,2},{7,3},{8,12},{9,13},{10,... | collective-permute-start | bytes 2654216 | tf_op jit(solution)/shard_map/ppermute | solution.py:315
  91.6 49.6 %collective-permute-start.14 = (bf16[96,4608]{1,0:T(8,128)(2,1)}, bf16[96,4608]{1,0:T(8,128)(2,1)S(1)}, u32[]{:S(2)}, u32[]{:S(2)}) collective-permute-start(bf16[96,4608]{1,0:T(8,128)(2,1)} %collective-permute-done.5.refs_1_), channel_id=1, source_target_pairs={{0,4},{1,5},{2,0},{3,1},{4,6},{5,7},{6,2},{7,3},{8,12},{9,13},{10,... | collective-permute-start | bytes 2654216 | tf_op jit(solution)/shard_map/ppermute | solution.py:315
  112.7 31.2 %collective-permute-start.18 = (bf16[96,4608]{1,0:T(8,128)(2,1)S(1)}, bf16[96,4608]{1,0:T(8,128)(2,1)S(1)}, u32[]{:S(2)}, u32[]{:S(2)}) collective-permute-start(bf16[96,4608]{1,0:T(8,128)(2,1)S(1)} %get-tuple-element.69), channel_id=1, source_target_pairs={{0,8},{1,9},{2,10},{3,11},{4,12},{5,13},{6,14},{7,15},{8,0},{9,1},... | collective-permute-start | bytes 2654216 | tf_op jit(solution)/shard_map/ppermute | solution.py:315
  113.6 52.1 %collective-permute-start.17 = (bf16[96,4608]{1,0:T(8,128)(2,1)S(1)}, bf16[96,4608]{1,0:T(8,128)(2,1)S(1)}, u32[]{:S(2)}, u32[]{:S(2)}) collective-permute-start(bf16[96,4608]{1,0:T(8,128)(2,1)S(1)} %collective-permute-done.10.refs_0_), channel_id=1, source_target_pairs={{0,4},{1,5},{2,0},{3,1},{4,6},{5,7},{6,2},{7,3},{8,12},{9,13},{10,... | collective-permute-start | bytes 2654216 | tf_op jit(solution)/shard_map/ppermute | solution.py:315
  120.5 23.3 %collective-permute-start.19 = (bf16[96,4608]{1,0:T(8,128)(2,1)S(1)}, bf16[96,4608]{1,0:T(8,128)(2,1)}, u32[]{:S(2)}, u32[]{:S(2)}) collective-permute-start(bf16[96,4608]{1,0:T(8,128)(2,1)S(1)} %get-tuple-element.78), channel_id=1, source_target_pairs={{0,16},{1,17},{2,18},{3,19},{4,20},{5,21},{6,22},{7,23},{8,24},{9,... | collective-permute-start | bytes 2654216 | tf_op jit(solution)/shard_map/ppermute | solution.py:315
  138.8 22.9 %collective-permute-start.20 = (bf16[96,4608]{1,0:T(8,128)(2,1)S(1)}, bf16[96,4608]{1,0:T(8,128)(2,1)}, u32[]{:S(2)}, u32[]{:S(2)}) collective-permute-start(bf16[96,4608]{1,0:T(8,128)(2,1)S(1)} %get-tuple-element.72), channel_id=1, source_target_pairs={{0,24},{1,25},{2,26},{3,27},{4,28},{5,29},{6,30},{7,31},{8,16},{9,... | collective-permute-start | bytes 2654216 | tf_op jit(solution)/shard_map/ppermute | solution.py:315
  141.2 36.9 %collective-permute-start.13 = (bf16[96,4608]{1,0:T(8,128)(2,1)}, bf16[96,4608]{1,0:T(8,128)(2,1)S(1)}, u32[]{:S(2)}, u32[]{:S(2)}) collective-permute-start(bf16[96,4608]{1,0:T(8,128)(2,1)} %collective-permute-done.9.refs_1_), channel_id=1, source_target_pairs={{0,4},{1,5},{2,0},{3,1},{4,6},{5,7},{6,2},{7,3},{8,12},{9,13},{10,... | collective-permute-start | bytes 2654216 | tf_op jit(solution)/shard_map/ppermute | solution.py:315
  158.6 49.5 %collective-permute-start.23 = (bf16[96,4608]{1,0:T(8,128)(2,1)S(1)}, bf16[96,4608]{1,0:T(8,128)(2,1)S(1)}, u32[]{:S(2)}, u32[]{:S(2)}) collective-permute-start(bf16[96,4608]{1,0:T(8,128)(2,1)S(1)} %get-tuple-element.80), channel_id=1, source_target_pairs={{0,8},{1,9},{2,10},{3,11},{4,12},{5,13},{6,14},{7,15},{8,0},{9,1},... | collective-permute-start | bytes 2654216 | tf_op jit(solution)/shard_map/ppermute | solution.py:315
  165.7 42.4 %collective-permute-start.21 = (bf16[96,4608]{1,0:T(8,128)(2,1)S(1)}, bf16[96,4608]{1,0:T(8,128)(2,1)S(1)}, u32[]{:S(2)}, u32[]{:S(2)}) collective-permute-start(bf16[96,4608]{1,0:T(8,128)(2,1)S(1)} %broadcast_select_fusion), channel_id=1, source_target_pairs={{0,2},{1,3},{2,0},{3,1},{4,6},{5,7},{6,4},{7,5},{8,10},{9,11},{10,... | collective-permute-start | bytes 2654216 | tf_op jit(solution)/shard_map/ppermute | solution.py:315
  178.1 32.0 %collective-permute-start.24 = (bf16[96,4608]{1,0:T(8,128)(2,1)S(1)}, bf16[96,4608]{1,0:T(8,128)(2,1)S(1)}, u32[]{:S(2)}, u32[]{:S(2)}) collective-permute-start(bf16[96,4608]{1,0:T(8,128)(2,1)S(1)} %get-tuple-element.86), channel_id=1, source_target_pairs={{0,16},{1,17},{2,18},{3,19},{4,20},{5,21},{6,22},{7,23},{8,24},{9,... | collective-permute-start | bytes 2654216 | tf_op jit(solution)/shard_map/ppermute | solution.py:315
  178.1 57.5 %collective-permute-start.15 = (bf16[96,4608]{1,0:T(8,128)(2,1)S(1)}, bf16[96,4608]{1,0:T(8,128)(2,1)S(1)}, u32[]{:S(2)}, u32[]{:S(2)}) collective-permute-start(bf16[96,4608]{1,0:T(8,128)(2,1)S(1)} %broadcast_select_fusion.2), channel_id=1, source_target_pairs={{0,2},{1,3},{2,0},{3,1},{4,6},{5,7},{6,4},{7,5},{8,10},{9,11},{10,... | collective-permute-start | bytes 2654216 | tf_op jit(solution)/shard_map/ppermute | solution.py:315
  193.0 57.5 %collective-permute-start.25 = (bf16[96,4608]{1,0:T(8,128)(2,1)S(1)}, bf16[96,4608]{1,0:T(8,128)(2,1)}, u32[]{:S(2)}, u32[]{:S(2)}) collective-permute-start(bf16[96,4608]{1,0:T(8,128)(2,1)S(1)} %get-tuple-element.83), channel_id=1, source_target_pairs={{0,24},{1,25},{2,26},{3,27},{4,28},{5,29},{6,30},{7,31},{8,16},{9,... | collective-permute-start | bytes 2654216 | tf_op jit(solution)/shard_map/ppermute | solution.py:315
  208.2 47.8 %collective-permute-start.26 = (bf16[96,4608]{1,0:T(8,128)(2,1)S(1)}, bf16[96,4608]{1,0:T(8,128)(2,1)S(1)}, u32[]{:S(2)}, u32[]{:S(2)}) collective-permute-start(bf16[96,4608]{1,0:T(8,128)(2,1)S(1)} %fusion.67), channel_id=1, source_target_pairs={{0,2},{1,3},{2,6},{3,7},{4,0},{5,1},{6,4},{7,5},{8,10},{9,11},{10,... | collective-permute-start | bytes 2654216 | tf_op jit(solution)/shard_map/ppermute | solution.py:315
  208.2 47.8 %collective-permute-start.22 = (bf16[96,4608]{1,0:T(8,128)(2,1)S(1)}, bf16[96,4608]{1,0:T(8,128)(2,1)S(1)}, u32[]{:S(2)}, u32[]{:S(2)}) collective-permute-start(bf16[96,4608]{1,0:T(8,128)(2,1)S(1)} %broadcast_select_fusion.1), channel_id=1, source_target_pairs={{0,2},{1,3},{2,0},{3,1},{4,6},{5,7},{6,4},{7,5},{8,10},{9,11},{10,... | collective-permute-start | bytes 2654216 | tf_op jit(solution)/shard_map/ppermute | solution.py:315
  289.9 33.0 %collective-permute-start.31 = (bf16[96,4608]{1,0:T(8,128)(2,1)S(1)}, bf16[96,4608]{1,0:T(8,128)(2,1)S(1)}, u32[]{:S(2)}, u32[]{:S(2)}) collective-permute-start(bf16[96,4608]{1,0:T(8,128)(2,1)S(1)} %fusion.75), channel_id=1, source_target_pairs={{0,4},{1,5},{2,0},{3,1},{4,6},{5,7},{6,2},{7,3},{8,12},{9,13},{10,... | collective-permute-start | bytes 2654216 | tf_op jit(solution)/shard_map/ppermute | solution.py:315
  (25 other events, 326.6 us)

commit v4 on v3

--- a/solution.py
+++ b/solution.py
@@ -298,13 +298,15 @@
     def back(row, m):
         return row ^ m if paired else (row + n_row - m) % n_row
 
-    def send(value, rows=0, hops=0, swap=0, reverse=False, route=None):
+    def send(value, rows=0, hops=0, swap=0, reverse=False, route=None, near=None):
         pairs = []
         for row in range(n_row):
             for chip in range(n_chip):
                 for core in range(CORES):
                     to_row = back(row, rows) if reverse else partner(row, rows)
                     to_chip = route[chip] if route else order[(place[chip] + hops) % n_chip]
+                    if near is not None and near != (abs(to_chip - chip) <= 1):
+                        continue
                     to_core = (core + swap) % CORES
                     pairs.append(
                         (
@@ -323,7 +325,8 @@
 
     def own_part(m):
         at = partner(row_at, m) * depth
-        return lax.dynamic_slice_in_dim(r_vector, at, depth, axis=1) * shrink[:, None]
+        source = r_vector if m < 2 else after(r_vector, mine[0, 0])
+        return lax.dynamic_slice_in_dim(source, at, depth, axis=1) * shrink[:, None]
 
     mine = {(0, 0): own_part(0)}
     for m in range(1, n_row):
@@ -412,12 +415,20 @@
         if g > 1:
             earlier += [arrived[at] for at in groups[g - 2] if at in arrived]
         for k in range(n_chip - 1):
-            if last_of[k] + 2 == g:
+            if last_of[k] + (2 if k < n_chip - 2 else 1) == g:
                 code = summed(k)
                 earlier.append(code)
-                codes[k] = send(code, hops=n_chip - k) if k > 0 else code
+                if k == 0:
+                    codes[k] = code
+                elif k < n_chip - 2:
+                    codes[k] = send(code, hops=n_chip - k)
+                else:
+                    near_code = send(code, hops=n_chip - k, near=True)
+                    far_code = code
         if n_row + g + 1 < sent and 0 < g <= n_row:
             earlier.append(mine[turns[n_row + g + 1]])
+        if g == len(groups) - 2 and n_chip > 2:
+            earlier.append(near_code)
         for k in range(1, n_chip - 1):
             if k in codes and k < n_chip - 2 and g == last_of[k] + 4:
                 earlier.append(codes[k])
@@ -444,7 +455,12 @@
             sent += 1
     s = n_chip - 1
     code = summed(s)
-    codes[s] = send(after(code, codes[n_chip - 2]), hops=n_chip - s)
+    if n_chip > 2:
+        far_code = after(far_code, mine[turns[-2]])
+        far_code = send(far_code, hops=2, near=False)
+        code = after(code, far_code)
+        codes[n_chip - 2] = near_code + far_code
+    codes[s] = send(code, hops=n_chip - s)
     early = [codes[k] for k in range(n_chip - 1)]
     late = [codes[s]]
     early[0] = after(early[0], code)
@@ -454,7 +470,7 @@
     rest, acc = add_sums(
         late, start_late, True, scalars, vir_row, acc, rest, r_vector, r_previous
     )
-    next_vector = next_rows(acc, rest, r_vector, out_width)
+    next_vector = next_rows(acc, rest, r_vector, CORES * out_width)
     both = acc.reshape(vectors, SUMS, 8, V)[:, 0, :2, 0].T
     whole = lax.dynamic_update_slice(
         jnp.zeros((2, NVEC), jnp.float32), both, (0, linear_index * vectors)

time: 354 us -> 335 us (0.946)
  waiting for transfers between devices: 76.1 us -> 65.7 us
  starting transfers between devices: 69.9 us -> 62.9 us
    ppermute x39 -> x40, waiting for transfers between devices: 76.1 us -> 65.7 us  [send(): return lax.ppermute(value, AXES, pairs)]
    ppermute x39 -> x40, starting transfers between devices: 69.9 us -> 62.9 us  [send(): return lax.ppermute(value, AXES, pairs)]
  transfers between devices with their start and end apart: 39 -> 40, of which waited for: 14 -> 15; matrix products, arithmetic and copies ran while one was open for 10% -> 11% of each run, Pallas kernels for 44% -> 46%
where the time goes in v4:
time: 335 us
  Pallas kernels  159 us (47%)
  waiting for transfers between devices  65.7 us (20%)
  starting transfers between devices  62.9 us (19%)
  other arithmetic  26.1 us (8%)
  local copies, waits for them, and re-layouts  13.1 us (4%)
  between operations  7.56 us (2%)
    pallas_call x9, Pallas kernels, product(): pl.pallas_call(functools.partial(product_kernel, coded), in_specs=[hbm] *...  139 us
    ppermute x40, waiting for transfers between devices, send(): return lax.ppermute(value, AXES, pairs)  65.7 us
    ppermute x40, starting transfers between devices, send(): return lax.ppermute(value, AXES, pairs)  62.9 us
    pallas_call x2, Pallas kernels, add_sums(): pl.pallas_call(functools.partial(sums_kernel, blocks, last), in_specs=[sm...  13.6 us
    convert_element_type x4, other arithmetic, encode(): return jnp.where(value < 0, -size, size).astype(jnp.bfloat16)  13.2 us
    pallas_call x1, Pallas kernels, next_rows(): pl.pallas_call(next_kernel, grid=(row_width // width,), in_specs=[pl.Bloc...  7.09 us
  transfers between devices with their start and end apart: 40, of which 15 were waited for; matrix products, arithmetic and copies ran while one was open for 11% of the time, Pallas kernels for 46%

profile of v4, /device:TPU:0, one launch (start us, length us, event | category | flops | bytes accessed | tf_op | source)
XLA Modules:
  0.0 334.6 jit_solution(3111329240477763816)
XLA Ops:
  16.1 13.4 %collective-permute-done.refs_0_ = bf16[96,4608]{1,0:T(8,128)(2,1)S(1)} collective-permute-done((bf16[96,4608]{1,0:T(8,128)(2,1)S(1)}, bf16[96,4608]{1,0:T(8,128)(2,1)S(1)}, u32[]{:S(2)}, u32[]{:S(2)}) %collective-permute-start) | collective-permute-done | bytes 884768 | tf_op jit(solution)/shard_map/ppermute | solution.py:317
  29.5 4.2 %collective-permute-done.1.refs_1_ = bf16[96,4608]{1,0:T(8,128)(2,1)S(1)} collective-permute-done((bf16[96,4608]{1,0:T(8,128)(2,1)S(1)}, bf16[96,4608]{1,0:T(8,128)(2,1)S(1)}, u32[]{:S(2)}, u32[]{:S(2)}) %collective-permute-start.1) | collective-permute-done | bytes 884768 | tf_op jit(solution)/shard_map/ppermute | solution.py:317
  55.9 14.8 %shard_map.121 = (bf16[96,4608]{1,0:T(8,128)(2,1)S(1)}, bf16[96,4608]{1,0:T(8,128)(2,1)S(1)}) custom-call(bf16[96,4608]{1,0:T(8,128)(2,1)S(1)} %collective-permute-done.refs_0_, bf16[96,4608]{1,0:T(8,128)(2,1)S(1)} %collective-permute-done.1.refs_1_, bf16[4608,2304]{1,0:T(8,128)(2,1)} %refs_1_.3, bf16[4608,2304]{1,0:T(8,128)(2,1)} %collective-permute-done.3.refs_3_.refs_2_, ...), custom_call_target="tpu_custom_call" | custom-call | flops 1769472 | bytes 1769472 | tf_op jit(solution)/shard_map/pallas_call | solution.py:108
  73.1 14.7 %shard_map.122 = (bf16[96,4608]{1,0:T(8,128)(2,1)S(1)}, f32[96,4608]{1,0:T(8,128)S(1)}) custom-call(bf16[96,4608]{1,0:T(8,128)(2,1)S(1)} %collective-permute-done.2.refs_0_, bf16[96,4608]{1,0:T(8,128)(2,1)S(1)} %get-tuple-element.107.refs_1_, bf16[4608,2304]{1,0:T(8,128)(2,1)} %refs_1_.3, bf16[4608,2304]{1,0:T(8,128)(2,1)} %collective-permute-done.3.refs_3_.refs_2_, ...), custom_call_target="tpu_custom_call" | custom-call | flops 1769472 | bytes 1769472 | tf_op jit(solution)/shard_map/pallas_call | solution.py:108
  95.3 18.2 %shard_map.123 = (bf16[96,4608]{1,0:T(8,128)(2,1)S(1)}, bf16[96,4608]{1,0:T(8,128)(2,1)S(1)}) custom-call(bf16[96,4608]{1,0:T(8,128)(2,1)S(1)} %collective-permute-done.11.refs_0_, bf16[96,4608]{1,0:T(8,128)(2,1)} %collective-permute-done.5.refs_1_, bf16[4608,2304]{1,0:T(8,128)(2,1)} %refs_1_.3, bf16[4608,2304]{1,0:T(8,128)(2,1)} %collective-permute-done.3.refs_3_.refs_2_, ...), custom_call_target="tpu_custom_call" | custom-call | flops 1769472 | bytes 1769472 | tf_op jit(solution)/shard_map/pallas_call | solution.py:108
  114.5 3.3 collective-permute-start.17
  117.8 3.6 %fusion.63.refs_0_ = bf16[96,4608]{1,0:T(8,128)(2,1)} fusion(bf16[96,4608]{1,0:T(8,128)(2,1)S(1)} %collective-permute-done.8, bf16[96,4608]{1,0:T(8,128)(2,1)S(1)} %collective-permute-done.7, f32[96,4608]{1,0:T(8,128)S(1)} %get-tuple-element.67, bf16[96,4608]{1,0:T(8,128)(2,1)S(1)} %collective-permute-done.6), kind=kLoop, calls=%fused_computation.104 | loop fusion | flops 16809984 | bytes 5308416 | tf_op jit(solution)/shard_map/convert_element_type | solution.py:27
  121.9 17.7 %shard_map.124 = (bf16[96,4608]{1,0:T(8,128)(2,1)S(1)}, f32[96,4608]{1,0:T(8,128)S(1)}) custom-call(bf16[96,4608]{1,0:T(8,128)(2,1)S(1)} %collective-permute-done.10.refs_0_, bf16[96,4608]{1,0:T(8,128)(2,1)} %collective-permute-done.9.refs_1_, bf16[4608,2304]{1,0:T(8,128)(2,1)} %refs_1_.3, bf16[4608,2304]{1,0:T(8,128)(2,1)} %collective-permute-done.3.refs_3_.refs_2_, ...), custom_call_target="tpu_custom_call" | custom-call | flops 1769472 | bytes 1769472 | tf_op jit(solution)/shard_map/pallas_call | solution.py:108
  144.7 14.8 %shard_map.125 = (bf16[96,4608]{1,0:T(8,128)(2,1)S(1)}, bf16[96,4608]{1,0:T(8,128)(2,1)S(1)}) custom-call(bf16[96,4608]{1,0:T(8,128)(2,1)S(1)} %collective-permute-done.12.refs_0_, bf16[96,4608]{1,0:T(8,128)(2,1)S(1)} %collective-permute-done.14.refs_1_, bf16[4608,2304]{1,0:T(8,128)(2,1)} %refs_1_.3, ...), custom_call_target="tpu_custom_call" | custom-call | flops 1769472 | bytes 1769472 | tf_op jit(solution)/shard_map/pallas_call | solution.py:108
  162.6 3.9 %fusion.67 = bf16[96,4608]{1,0:T(8,128)(2,1)S(1)} fusion(bf16[96,4608]{1,0:T(8,128)(2,1)} %collective-permute-done.20, bf16[96,4608]{1,0:T(8,128)(2,1)S(1)} %collective-permute-done.19, f32[96,4608]{1,0:T(8,128)S(1)} %get-tuple-element.84, bf16[96,4608]{1,0:T(8,128)(2,1)S(1)} %collective-permute-done.18), kind=kLoop, calls=%fused_computation.108 | loop fusion | flops 16809984 | bytes 5308416 | tf_op jit(solution)/shard_map/convert_element_type | solution.py:27
  166.5 12.3 %collective-permute-start.27 = (bf16[96,4608]{1,0:T(8,128)(2,1)S(1)}, bf16[96,4608]{1,0:T(8,128)(2,1)S(1)}, u32[]{:S(2)}, u32[]{:S(2)}) collective-permute-start(bf16[96,4608]{1,0:T(8,128)(2,1)S(1)} %fusion.67), channel_id=1, source_target_pairs={{0,2},{1,3},{2,6},{3,7},{4,0},{5,1},{6,4},{7,5},{8,10},{9,11},{10,... | collective-permute-start | bytes 2654216 | tf_op jit(solution)/shard_map/ppermute | solution.py:317
  178.8 14.7 %shard_map.126 = (bf16[96,4608]{1,0:T(8,128)(2,1)S(1)}, f32[96,4608]{1,0:T(8,128)S(1)}) custom-call(bf16[96,4608]{1,0:T(8,128)(2,1)S(1)} %collective-permute-done.17.refs_0_, bf16[96,4608]{1,0:T(8,128)(2,1)S(1)} %collective-permute-done.13.refs_1_, bf16[4608,2304]{1,0:T(8,128)(2,1)} %refs_1_.3, bf16[4608,2304]{1,0:T(8,128)(2,1)} %collective-permute-done.3.refs_3_.refs_2_, ...), custom_call_target="tpu_custom_call" | custom-call | flops 1769472 | bytes 1769472 | tf_op jit(solution)/shard_map/pallas_call | solution.py:108
  193.6 3.0 collective-permute-start.25
  197.4 11.4 %collective-permute-done.21.refs_0_ = bf16[96,4608]{1,0:T(8,128)(2,1)S(1)} collective-permute-done((bf16[96,4608]{1,0:T(8,128)(2,1)S(1)}, bf16[96,4608]{1,0:T(8,128)(2,1)S(1)}, u32[]{:S(2)}, u32[]{:S(2)}) %collective-permute-start.21) | collective-permute-done | bytes 884768 | tf_op jit(solution)/shard_map/ppermute | solution.py:317
  211.3 2.9 fusion.71
  215.9 16.0 %collective-permute-done.15.refs_1_ = bf16[96,4608]{1,0:T(8,128)(2,1)S(1)} collective-permute-done((bf16[96,4608]{1,0:T(8,128)(2,1)S(1)}, bf16[96,4608]{1,0:T(8,128)(2,1)S(1)}, u32[]{:S(2)}, u32[]{:S(2)}) %collective-permute-start.15) | collective-permute-done | bytes 884768 | tf_op jit(solution)/shard_map/ppermute | solution.py:317
  231.8 14.8 %shard_map.127 = (bf16[96,4608]{1,0:T(8,128)(2,1)S(1)}, bf16[96,4608]{1,0:T(8,128)(2,1)S(1)}) custom-call(bf16[96,4608]{1,0:T(8,128)(2,1)S(1)} %collective-permute-done.21.refs_0_, bf16[96,4608]{1,0:T(8,128)(2,1)S(1)} %collective-permute-done.15.refs_1_, bf16[4608,2304]{1,0:T(8,128)(2,1)} %refs_1_.3, ...), custom_call_target="tpu_custom_call" | custom-call | flops 1769472 | bytes 1769472 | tf_op jit(solution)/shard_map/pallas_call | solution.py:108
  250.3 14.5 %shard_map.128 = bf16[96,4608]{1,0:T(8,128)(2,1)S(1)} custom-call(bf16[96,4608]{1,0:T(8,128)(2,1)S(1)} %collective-permute-done.22.refs_0_, bf16[4608,2304]{1,0:T(8,128)(2,1)} %refs_1_.3, bf16[4608,2304]{1,0:T(8,128)(2,1)} %collective-permute-done.3.refs_3_.refs_2_, bf16[576,576]{1,0:T(8,128)(2,1)S(1)} %constant_dynamic-update-slice_fusion.refs_4_.refs_3_), custom_call_target="tpu_custom_call" | custom-call | flops 884736 | bytes 884736 | tf_op jit(solution)/shard_map/pallas_call | solution.py:108
  271.0 14.4 %shard_map.129 = f32[96,4608]{1,0:T(8,128)S(1)} custom-call(bf16[96,4608]{1,0:T(8,128)(2,1)S(1)} %collective-permute-done.16.refs_0_, bf16[4608,2304]{1,0:T(8,128)(2,1)} %refs_1_.3, bf16[4608,2304]{1,0:T(8,128)(2,1)} %collective-permute-done.3.refs_3_.refs_2_, bf16[576,576]{1,0:T(8,128)(2,1)S(1)} %constant_dynamic-update-slice_fusion.refs_4_.refs_3_), custom_call_target="tpu_custom_call" | custom-call | flops 884736 | bytes 884736 | tf_op jit(solution)/shard_map/pallas_call | solution.py:108
  285.4 2.9 fusion.75
  290.5 8.3 %shard_map.130 = (f32[96,18432]{1,0:T(8,128)}, f32[6,8,384]{2,1,0:T(8,128)}) custom-call(s32[6]{0:T(128)} %stack.35.starts, f32[48]{0:T(128)} %occ.1, f32[2]{0:T(128)} %get-tuple-element.55.grow, f32[2]{0:T(128)} %copy-done.4, f32[2]{0:T(128)} %dynamic_slice.43.beta_prev, f32[1,384]{1,0:T(1,128)} %broadcast_in_dim.13.vir_ref, ...), custom_call_target="tpu_custom_call" | custom-call | flops 39813120 | bytes 13271040 | tf_op jit(solution)/shard_map/pallas_call | solution.py:221
  298.8 8.7 %collective-permute-done.32.refs_1_ = bf16[96,4608]{1,0:T(8,128)(2,1)S(1)} collective-permute-done((bf16[96,4608]{1,0:T(8,128)(2,1)S(1)}, bf16[96,4608]{1,0:T(8,128)(2,1)S(1)}, u32[]{:S(2)}, u32[]{:S(2)}) %collective-permute-start.32) | collective-permute-done | bytes 884768 | tf_op jit(solution)/shard_map/ppermute | solution.py:317
  308.4 5.3 %shard_map.131 = (f32[96,18432]{1,0:T(8,128)}, f32[6,8,384]{2,1,0:T(8,128)}) custom-call(s32[2]{0:T(128)} %pad_add_fusion.starts, f32[48]{0:T(128)} %occ.1, f32[2]{0:T(128)} %get-tuple-element.55.grow, f32[2]{0:T(128)} %copy-done.4, f32[2]{0:T(128)} %dynamic_slice.43.beta_prev, f32[1,384]{1,0:T(1,128)} %broadcast_in_dim.13.vir_ref, ...), custom_call_target="tpu_custom_call", output_to_operand_aliasing={{0}: (9, {})} | custom-call | flops 13271040 | bytes 4423680 | tf_op jit(solution)/shard_map/pallas_call | solution.py:221
  326.7 7.1 %shard_map.132 = bf16[96,18432]{1,0:T(8,128)(2,1)} custom-call(f32[6,8,384]{2,1,0:T(8,128)} %get-tuple-element.101.acc_ref, f32[96,18432]{1,0:T(8,128)} %get-tuple-element.102.rest_ref, bf16[96,18432]{1,0:T(8,128)(2,1)} %r_ref.5), custom_call_target="tpu_custom_call" | custom-call | flops 10616832 | bytes 14155776 | tf_op jit(solution)/shard_map/pallas_call | solution.py:256
  (123 shorter events, 82.2 us)
Async XLA Ops:
  0.6 55.3 %collective-permute-start.3 = (bf16[4608,2304]{1,0:T(8,128)(2,1)}, bf16[4608,2304]{1,0:T(8,128)(2,1)}, u32[]{:S(2)}, u32[]{:S(2)}) collective-permute-start(bf16[4608,2304]{1,0:T(8,128)(2,1)} %refs_1_.3), channel_id=1, source_target_pairs={{0,1},{1,0},{2,3},{3,2},{4,5},{5,4},{6,7},{7,6},{8,9},{9,8},{10,11... | collective-permute-start | bytes 63701000 | tf_op jit(solution)/shard_map/ppermute | solution.py:317
  6.7 22.9 %collective-permute-start = (bf16[96,4608]{1,0:T(8,128)(2,1)S(1)}, bf16[96,4608]{1,0:T(8,128)(2,1)S(1)}, u32[]{:S(2)}, u32[]{:S(2)}) collective-permute-start(bf16[96,4608]{1,0:T(8,128)(2,1)S(1)} %get-tuple-element.108), channel_id=1, source_target_pairs={{0,8},{1,9},{2,10},{3,11},{4,12},{5,13},{6,14},{7,15},{8,0},{9,1},... | collective-permute-start | bytes 2654216 | tf_op jit(solution)/shard_map/ppermute | solution.py:317
  13.6 57.7 %collective-permute-start.9 = (bf16[96,4608]{1,0:T(8,128)(2,1)S(1)}, bf16[96,4608]{1,0:T(8,128)(2,1)}, u32[]{:S(2)}, u32[]{:S(2)}) collective-permute-start(bf16[96,4608]{1,0:T(8,128)(2,1)S(1)} %get-tuple-element.107.refs_1_), channel_id=1, source_target_pairs={{0,4},{1,5},{2,0},{3,1},{4,6},{5,7},{6,2},{7,3},{8,12},{9,13},{10,... | collective-permute-start | bytes 2654216 | tf_op jit(solution)/shard_map/ppermute | solution.py:317
  33.8 39.0 %collective-permute-start.2 = (bf16[96,4608]{1,0:T(8,128)(2,1)}, bf16[96,4608]{1,0:T(8,128)(2,1)S(1)}, u32[]{:S(2)}, u32[]{:S(2)}) collective-permute-start(bf16[96,4608]{1,0:T(8,128)(2,1)} %get-tuple-element.62), channel_id=1, source_target_pairs={{0,24},{1,25},{2,26},{3,27},{4,28},{5,29},{6,30},{7,31},{8,16},{9,... | collective-permute-start | bytes 2654216 | tf_op jit(solution)/shard_map/ppermute | solution.py:317
  35.3 37.8 %collective-permute-start.5 = (bf16[96,4608]{1,0:T(8,128)(2,1)S(1)}, bf16[96,4608]{1,0:T(8,128)(2,1)}, u32[]{:S(2)}, u32[]{:S(2)}) collective-permute-start(bf16[96,4608]{1,0:T(8,128)(2,1)S(1)} %collective-permute-done.1.refs_1_), channel_id=1, source_target_pairs={{0,4},{1,5},{2,0},{3,1},{4,6},{5,7},{6,2},{7,3},{8,12},{9,13},{10,... | collective-permute-start | bytes 2654216 | tf_op jit(solution)/shard_map/ppermute | solution.py:317
  53.3 36.8 %collective-permute-start.11 = (bf16[96,4608]{1,0:T(8,128)(2,1)S(1)}, bf16[96,4608]{1,0:T(8,128)(2,1)S(1)}, u32[]{:S(2)}, u32[]{:S(2)}) collective-permute-start(bf16[96,4608]{1,0:T(8,128)(2,1)S(1)} %collective-permute-done.refs_0_), channel_id=1, source_target_pairs={{0,4},{1,5},{2,0},{3,1},{4,6},{5,7},{6,2},{7,3},{8,12},{9,13},{10,... | collective-permute-start | bytes 2654216 | tf_op jit(solution)/shard_map/ppermute | solution.py:317
  70.7 21.8 %collective-permute-start.7 = (bf16[96,4608]{1,0:T(8,128)(2,1)S(1)}, bf16[96,4608]{1,0:T(8,128)(2,1)S(1)}, u32[]{:S(2)}, u32[]{:S(2)}) collective-permute-start(bf16[96,4608]{1,0:T(8,128)(2,1)S(1)} %get-tuple-element.68), channel_id=1, source_target_pairs={{0,16},{1,17},{2,18},{3,19},{4,20},{5,21},{6,22},{7,23},{8,24},{9,... | collective-permute-start | bytes 2654216 | tf_op jit(solution)/shard_map/ppermute | solution.py:317
  71.3 22.5 %collective-permute-start.6 = (bf16[96,4608]{1,0:T(8,128)(2,1)S(1)}, bf16[96,4608]{1,0:T(8,128)(2,1)S(1)}, u32[]{:S(2)}, u32[]{:S(2)}) collective-permute-start(bf16[96,4608]{1,0:T(8,128)(2,1)S(1)} %get-tuple-element.65), channel_id=1, source_target_pairs={{0,8},{1,9},{2,10},{3,11},{4,12},{5,13},{6,14},{7,15},{8,0},{9,1},... | collective-permute-start | bytes 2654216 | tf_op jit(solution)/shard_map/ppermute | solution.py:317
  72.8 22.6 %collective-permute-start.10 = (bf16[96,4608]{1,0:T(8,128)(2,1)S(1)}, bf16[96,4608]{1,0:T(8,128)(2,1)S(1)}, u32[]{:S(2)}, u32[]{:S(2)}) collective-permute-start(bf16[96,4608]{1,0:T(8,128)(2,1)S(1)} %collective-permute-done.2.refs_0_), channel_id=1, source_target_pairs={{0,4},{1,5},{2,0},{3,1},{4,6},{5,7},{6,2},{7,3},{8,12},{9,13},{10,... | collective-permute-start | bytes 2654216 | tf_op jit(solution)/shard_map/ppermute | solution.py:317
  87.9 29.9 %collective-permute-start.8 = (bf16[96,4608]{1,0:T(8,128)(2,1)S(1)}, bf16[96,4608]{1,0:T(8,128)(2,1)S(1)}, u32[]{:S(2)}, u32[]{:S(2)}) collective-permute-start(bf16[96,4608]{1,0:T(8,128)(2,1)S(1)} %get-tuple-element.69), channel_id=1, source_target_pairs={{0,24},{1,25},{2,26},{3,27},{4,28},{5,29},{6,30},{7,31},{8,16},{9,... | collective-permute-start | bytes 2654216 | tf_op jit(solution)/shard_map/ppermute | solution.py:317
  90.0 31.4 %collective-permute-start.12 = (bf16[96,4608]{1,0:T(8,128)(2,1)S(1)}, bf16[96,4608]{1,0:T(8,128)(2,1)S(1)}, u32[]{:S(2)}, u32[]{:S(2)}) collective-permute-start(bf16[96,4608]{1,0:T(8,128)(2,1)S(1)} %collective-permute-done.11.refs_0_), channel_id=1, source_target_pairs={{0,4},{1,5},{2,0},{3,1},{4,6},{5,7},{6,2},{7,3},{8,12},{9,13},{10,... | collective-permute-start | bytes 2654216 | tf_op jit(solution)/shard_map/ppermute | solution.py:317
  92.6 49.4 %collective-permute-start.14 = (bf16[96,4608]{1,0:T(8,128)(2,1)}, bf16[96,4608]{1,0:T(8,128)(2,1)S(1)}, u32[]{:S(2)}, u32[]{:S(2)}) collective-permute-start(bf16[96,4608]{1,0:T(8,128)(2,1)} %collective-permute-done.5.refs_1_), channel_id=1, source_target_pairs={{0,4},{1,5},{2,0},{3,1},{4,6},{5,7},{6,2},{7,3},{8,12},{9,13},{10,... | collective-permute-start | bytes 2654216 | tf_op jit(solution)/shard_map/ppermute | solution.py:317
  113.6 31.1 %collective-permute-start.18 = (bf16[96,4608]{1,0:T(8,128)(2,1)S(1)}, bf16[96,4608]{1,0:T(8,128)(2,1)S(1)}, u32[]{:S(2)}, u32[]{:S(2)}) collective-permute-start(bf16[96,4608]{1,0:T(8,128)(2,1)S(1)} %get-tuple-element.72), channel_id=1, source_target_pairs={{0,8},{1,9},{2,10},{3,11},{4,12},{5,13},{6,14},{7,15},{8,0},{9,1},... | collective-permute-start | bytes 2654216 | tf_op jit(solution)/shard_map/ppermute | solution.py:317
  114.5 64.3 %collective-permute-start.17 = (bf16[96,4608]{1,0:T(8,128)(2,1)S(1)}, bf16[96,4608]{1,0:T(8,128)(2,1)S(1)}, u32[]{:S(2)}, u32[]{:S(2)}) collective-permute-start(bf16[96,4608]{1,0:T(8,128)(2,1)S(1)} %collective-permute-done.10.refs_0_), channel_id=1, source_target_pairs={{0,4},{1,5},{2,0},{3,1},{4,6},{5,7},{6,2},{7,3},{8,12},{9,13},{10,... | collective-permute-start | bytes 2654216 | tf_op jit(solution)/shard_map/ppermute | solution.py:317
  121.4 23.3 %collective-permute-start.19 = (bf16[96,4608]{1,0:T(8,128)(2,1)S(1)}, bf16[96,4608]{1,0:T(8,128)(2,1)S(1)}, u32[]{:S(2)}, u32[]{:S(2)}) collective-permute-start(bf16[96,4608]{1,0:T(8,128)(2,1)S(1)} %get-tuple-element.81), channel_id=1, source_target_pairs={{0,16},{1,17},{2,18},{3,19},{4,20},{5,21},{6,22},{7,23},{8,24},{9,... | collective-permute-start | bytes 2654216 | tf_op jit(solution)/shard_map/ppermute | solution.py:317
  139.7 22.9 %collective-permute-start.20 = (bf16[96,4608]{1,0:T(8,128)(2,1)S(1)}, bf16[96,4608]{1,0:T(8,128)(2,1)}, u32[]{:S(2)}, u32[]{:S(2)}) collective-permute-start(bf16[96,4608]{1,0:T(8,128)(2,1)S(1)} %get-tuple-element.75), channel_id=1, source_target_pairs={{0,24},{1,25},{2,26},{3,27},{4,28},{5,29},{6,30},{7,31},{8,16},{9,... | collective-permute-start | bytes 2654216 | tf_op jit(solution)/shard_map/ppermute | solution.py:317
  142.0 36.9 %collective-permute-start.13 = (bf16[96,4608]{1,0:T(8,128)(2,1)}, bf16[96,4608]{1,0:T(8,128)(2,1)S(1)}, u32[]{:S(2)}, u32[]{:S(2)}) collective-permute-start(bf16[96,4608]{1,0:T(8,128)(2,1)} %collective-permute-done.9.refs_1_), channel_id=1, source_target_pairs={{0,4},{1,5},{2,0},{3,1},{4,6},{5,7},{6,2},{7,3},{8,12},{9,13},{10,... | collective-permute-start | bytes 2654216 | tf_op jit(solution)/shard_map/ppermute | solution.py:317
  159.5 51.8 %collective-permute-start.23 = (bf16[96,4608]{1,0:T(8,128)(2,1)S(1)}, bf16[96,4608]{1,0:T(8,128)(2,1)S(1)}, u32[]{:S(2)}, u32[]{:S(2)}) collective-permute-start(bf16[96,4608]{1,0:T(8,128)(2,1)S(1)} %get-tuple-element.83), channel_id=1, source_target_pairs={{0,8},{1,9},{2,10},{3,11},{4,12},{5,13},{6,14},{7,15},{8,0},{9,1},... | collective-permute-start | bytes 2654216 | tf_op jit(solution)/shard_map/ppermute | solution.py:317
  166.5 82.3 %collective-permute-start.27 = (bf16[96,4608]{1,0:T(8,128)(2,1)S(1)}, bf16[96,4608]{1,0:T(8,128)(2,1)S(1)}, u32[]{:S(2)}, u32[]{:S(2)}) collective-permute-start(bf16[96,4608]{1,0:T(8,128)(2,1)S(1)} %fusion.67), channel_id=1, source_target_pairs={{0,2},{1,3},{2,6},{3,7},{4,0},{5,1},{6,4},{7,5},{8,10},{9,11},{10,... | collective-permute-start | bytes 2654216 | tf_op jit(solution)/shard_map/ppermute | solution.py:317
  178.8 30.0 %collective-permute-start.21 = (bf16[96,4608]{1,0:T(8,128)(2,1)S(1)}, bf16[96,4608]{1,0:T(8,128)(2,1)S(1)}, u32[]{:S(2)}, u32[]{:S(2)}) collective-permute-start(bf16[96,4608]{1,0:T(8,128)(2,1)S(1)} %broadcast_select_fusion), channel_id=1, source_target_pairs={{0,2},{1,3},{2,0},{3,1},{4,6},{5,7},{6,4},{7,5},{8,10},{9,11},{10,... | collective-permute-start | bytes 2654216 | tf_op jit(solution)/shard_map/ppermute | solution.py:317
  178.8 32.5 %collective-permute-start.24 = (bf16[96,4608]{1,0:T(8,128)(2,1)S(1)}, bf16[96,4608]{1,0:T(8,128)(2,1)S(1)}, u32[]{:S(2)}, u32[]{:S(2)}) collective-permute-start(bf16[96,4608]{1,0:T(8,128)(2,1)S(1)} %get-tuple-element.89), channel_id=1, source_target_pairs={{0,16},{1,17},{2,18},{3,19},{4,20},{5,21},{6,22},{7,23},{8,24},{9,... | collective-permute-start | bytes 2654216 | tf_op jit(solution)/shard_map/ppermute | solution.py:317
  208.8 23.0 %collective-permute-start.15 = (bf16[96,4608]{1,0:T(8,128)(2,1)S(1)}, bf16[96,4608]{1,0:T(8,128)(2,1)S(1)}, u32[]{:S(2)}, u32[]{:S(2)}) collective-permute-start(bf16[96,4608]{1,0:T(8,128)(2,1)S(1)} %broadcast_select_fusion.2), channel_id=1, source_target_pairs={{0,2},{1,3},{2,0},{3,1},{4,6},{5,7},{6,4},{7,5},{8,10},{9,11},{10,... | collective-permute-start | bytes 2654216 | tf_op jit(solution)/shard_map/ppermute | solution.py:317
  211.3 39.0 %collective-permute-start.22 = (bf16[96,4608]{1,0:T(8,128)(2,1)S(1)}, bf16[96,4608]{1,0:T(8,128)(2,1)S(1)}, u32[]{:S(2)}, u32[]{:S(2)}) collective-permute-start(bf16[96,4608]{1,0:T(8,128)(2,1)S(1)} %broadcast_select_fusion.1), channel_id=1, source_target_pairs={{0,2},{1,3},{2,0},{3,1},{4,6},{5,7},{6,4},{7,5},{8,10},{9,11},{10,... | collective-permute-start | bytes 2654216 | tf_op jit(solution)/shard_map/ppermute | solution.py:317
  214.2 36.1 %collective-permute-start.26 = (bf16[96,4608]{1,0:T(8,128)(2,1)S(1)}, bf16[96,4608]{1,0:T(8,128)(2,1)S(1)}, u32[]{:S(2)}, u32[]{:S(2)}) collective-permute-start(bf16[96,4608]{1,0:T(8,128)(2,1)S(1)} %fusion.71), channel_id=1, source_target_pairs={{2,4},{3,5},{4,2},{5,3},{10,12},{11,13},{12,10},{13,11},{18,20},{1... | collective-permute-start | bytes 2654216 | tf_op jit(solution)/shard_map/ppermute | solution.py:317
  (25 other events, 317.5 us)
